TPU v7x, 128 devices: a whole 4x4x4 slice. The times are simulated.
128 devices in a mesh: seq: 16 (over y, z_hi, core), batch: 8 (over z_lo, x).
Axes of the slice: x: 4, y: 4, z: 4 (z_hi: 2, z_lo: 2; z = z_hi * 2 + z_lo), core: 2. Of those that a mesh axis runs over, the one named last changes fastest.
Arguments:
- tokens: bfloat16 [8, 4096, 768], P('batch', 'seq'), may hold values from -6 to 6
- cotangent: bfloat16 [8, 4096, 768], P('batch', 'seq'), may hold values from -6 to 6
- ln1_gain: float32 [768], replicated, may hold values from 0.1 to 1.9
- ln1_shift: float32 [768], replicated, may hold values from -3 to 3
- w_qkv: bfloat16 [768, 2304], replicated, may hold values from -0.3125 to 0.3125
- b_query: float32 [768], replicated, may hold values from -3 to 3
- b_value: float32 [768], replicated, may hold values from -3 to 3
- w_out: bfloat16 [768, 768], replicated, may hold values from -0.875 to 0.875
- b_out: float32 [768], replicated, may hold values from -3 to 3
- ln2_gain: float32 [768], replicated, may hold values from 0.1 to 1.9
- ln2_shift: float32 [768], replicated, may hold values from -3 to 3
- w_up: bfloat16 [768, 3072], replicated, may hold values from -0.21875 to 0.21875
- b_up: float32 [3072], replicated, may hold values from -3 to 3
- w_down: bfloat16 [3072, 768], replicated, may hold values from -0.109375 to 0.109375
- b_down: float32 [768], replicated, may hold values from -3 to 3
Outputs:
- output: bfloat16 [8, 4096, 768], P('batch', 'seq')
- grad_tokens: float32 [8, 4096, 768], P('batch', 'seq')
- grad_ln1_gain: float32 [768], replicated
- grad_ln1_shift: float32 [768], replicated
- grad_w_qkv: float32 [768, 2304], replicated
- grad_b_query: float32 [768], replicated
- grad_b_value: float32 [768], replicated
- grad_w_out: float32 [768, 768], replicated
- grad_b_out: float32 [768], replicated
- grad_ln2_gain: float32 [768], replicated
- grad_ln2_shift: float32 [768], replicated
- grad_w_up: float32 [768, 3072], replicated
- grad_b_up: float32 [3072], replicated
- grad_w_down: float32 [3072, 768], replicated
- grad_b_down: float32 [768], replicated
All inputs are finite; a program needn't handle non-finite values.
Results may differ from a plain program's by a relative error of at most 0.019.
Values may be sent and summed in bfloat16 or wider, within the bound.
No kernel may reach another device: no remote copies, remote signals or barrier semaphores. Data moves between devices by JAX's collectives and lax.ppermute only.
A program may use at most 192 MiB of HBM per device.

v0:
```python
import jax
import jax.numpy as jnp
from jax import lax
from jax.sharding import PartitionSpec as P

H = 12
HD = 64


masked_fill = -1e30


def layer_norm(values, gain, shift):
    center = values - jnp.mean(values, axis=-1, keepdims=True)
    spread = jnp.mean(center * center, axis=-1, keepdims=True)
    return center * lax.rsqrt(spread + 1e-05) * gain + shift


def block_scores(query_heads, key_heads, query_pos, key_pos):
    scores = (
        jnp.einsum("qhd,khd->hqk", query_heads, key_heads, preferred_element_type=jnp.float32)
        * 0.125
    )
    allowed = (key_pos[None, :] <= query_pos[:, None])[None]
    return (jnp.where(allowed, scores, masked_fill), allowed)


def score_grads(
    query_heads, grad_heads, log_total, delta, key_heads, value_heads, query_pos, key_pos
):
    scores, allowed = block_scores(query_heads, key_heads, query_pos, key_pos)
    probs = jnp.where(allowed, jnp.exp(scores - log_total[..., None]), 0.0)
    grad_probs = jnp.einsum(
        "qhd,khd->hqk", grad_heads, value_heads, preferred_element_type=jnp.float32
    )
    grad_scores = (probs * (grad_probs - delta[..., None])).astype(jnp.bfloat16)
    return (probs.astype(jnp.bfloat16), grad_scores)


def over_blocks(piece, rows, carry, active, work):
    blocks = piece.reshape(piece.shape[0] // rows, rows, piece.shape[1])
    firsts = jnp.arange(blocks.shape[0], dtype=jnp.int32) * rows

    def step(state, item):
        block, first = item
        return (
            lax.cond(
                active(first), lambda inner: work(inner, block, first), lambda inner: inner, state
            ),
            None,
        )

    result, _ = lax.scan(step, carry, (blocks, firsts))
    return result


def shards(
    tokens,
    cotangent,
    ln1_gain,
    ln1_shift,
    w_qkv,
    b_query,
    b_value,
    w_out,
    b_out,
    ln2_gain,
    ln2_shift,
    w_up,
    b_up,
    w_down,
    b_down,
):
    width = w_out.shape[0]
    rows = tokens.shape[1]
    rank = lax.axis_index("seq")
    offsets = jnp.arange(rows, dtype=jnp.int32)
    row_pos = rank * rows + offsets
    last_pos = rank * rows + rows - 1
    inputs = tokens[0].astype(jnp.float32)
    normed_one, back_one = jax.vjp(layer_norm, inputs, ln1_gain, ln1_shift)
    hidden_one = normed_one.astype(jnp.bfloat16)
    bias_full = jnp.concatenate([b_query, jnp.zeros((width,), jnp.float32), b_value])
    projected = (jnp.dot(hidden_one, w_qkv, preferred_element_type=jnp.float32) + bias_full).astype(
        jnp.bfloat16
    )
    queries = projected[:, :width]
    keys_values = projected[:, width:]
    query_heads = queries.reshape(rows, H, HD)

    def forward_work(state, block, first):
        run_max, run_total, totals = state
        key_heads = block[:, :width].reshape(rows, H, HD)
        value_heads = block[:, width:].reshape(rows, H, HD)
        scores, allowed = block_scores(query_heads, key_heads, row_pos, first + offsets)
        new_max = jnp.maximum(run_max, jnp.max(scores, axis=-1))
        weights = jnp.where(allowed, jnp.exp(scores - new_max[..., None]), 0.0)
        factor = jnp.exp(run_max - new_max)
        run_total = run_total * factor + jnp.sum(weights, axis=-1)
        totals = totals * factor[..., None] + jnp.einsum(
            "hqk,khd->hqd",
            weights.astype(jnp.bfloat16),
            value_heads,
            preferred_element_type=jnp.float32,
        )
        return (new_max, run_total, totals)

    start_state = (
        jnp.full((H, rows), masked_fill, jnp.float32),
        jnp.zeros((H, rows), jnp.float32),
        jnp.zeros((H, rows, HD), jnp.float32),
    )
    run_max, run_total, totals = over_blocks(
        lax.all_gather(keys_values, "seq", axis=0, tiled=True),
        rows,
        start_state,
        lambda first: first <= last_pos,
        forward_work,
    )
    attended_heads = jnp.transpose(totals / run_total[..., None], (1, 0, 2))
    log_total = run_max + jnp.log(run_total)
    attended = attended_heads.reshape(rows, width).astype(jnp.bfloat16)
    middle = inputs + jnp.dot(attended, w_out, preferred_element_type=jnp.float32) + b_out
    normed_two, back_two = jax.vjp(layer_norm, middle, ln2_gain, ln2_shift)
    hidden_two = normed_two.astype(jnp.bfloat16)
    inner = jnp.dot(hidden_two, w_up, preferred_element_type=jnp.float32) + b_up
    activated, back_gelu = jax.vjp(lambda value: jax.nn.gelu(value, approximate=True), inner)
    activated_low = activated.astype(jnp.bfloat16)
    result = middle + jnp.dot(activated_low, w_down, preferred_element_type=jnp.float32) + b_down
    seed_low = cotangent[0]
    seed = seed_low.astype(jnp.float32)
    grad_w_down = jnp.dot(activated_low.T, seed_low, preferred_element_type=jnp.float32)
    grad_b_down = jnp.sum(seed, axis=0)
    grad_act = jnp.dot(seed_low, w_down.T, preferred_element_type=jnp.float32)
    grad_inner = back_gelu(grad_act)[0].astype(jnp.bfloat16)
    grad_w_up = jnp.dot(hidden_two.T, grad_inner, preferred_element_type=jnp.float32)
    grad_b_up = jnp.sum(grad_inner.astype(jnp.float32), axis=0)
    grad_hidden_two = jnp.dot(grad_inner, w_up.T, preferred_element_type=jnp.float32)
    grad_mid_norm, grad_gain_two, grad_shift_two = back_two(grad_hidden_two)
    grad_middle = seed + grad_mid_norm
    grad_branch = grad_middle.astype(jnp.bfloat16)
    grad_w_out = jnp.dot(attended.T, grad_branch, preferred_element_type=jnp.float32)
    grad_b_out = jnp.sum(grad_branch.astype(jnp.float32), axis=0)
    grad_attended = jnp.dot(grad_branch, w_out.T, preferred_element_type=jnp.float32).astype(
        jnp.bfloat16
    )
    grad_heads = grad_attended.reshape(rows, H, HD)
    delta = jnp.einsum("qhd,qhd->hq", grad_heads.astype(jnp.float32), attended_heads)
    length = rows * lax.axis_size("seq")

    def return_work(state, block, first):
        grad_query, grad_kv = state
        key_heads = block[:, :width].reshape(rows, H, HD)
        value_heads = block[:, width:].reshape(rows, H, HD)
        probs_low, grad_scores = score_grads(
            query_heads,
            grad_heads,
            log_total,
            delta,
            key_heads,
            value_heads,
            row_pos,
            first + offsets,
        )
        grad_query = (
            grad_query
            + jnp.einsum("hqk,khd->hqd", grad_scores, key_heads, preferred_element_type=jnp.float32)
            * 0.125
        )
        grad_key = (
            jnp.einsum("hqk,qhd->khd", grad_scores, query_heads, preferred_element_type=jnp.float32)
            * 0.125
        )
        grad_value = jnp.einsum(
            "hqk,qhd->khd", probs_low, grad_heads, preferred_element_type=jnp.float32
        )
        update = jnp.concatenate(
            [grad_key.reshape(rows, width), grad_value.reshape(rows, width)], axis=1
        )
        current = lax.dynamic_slice_in_dim(grad_kv, first, rows, 0)
        grad_kv = lax.dynamic_update_slice_in_dim(grad_kv, current + update, first, 0)
        return (grad_query, grad_kv)

    start_back = (
        jnp.zeros((H, rows, HD), jnp.float32),
        jnp.zeros((length, 2 * width), jnp.float32),
    )
    grad_query, grad_kv = over_blocks(
        lax.all_gather(keys_values, "seq", axis=0, tiled=True),
        rows,
        start_back,
        lambda first: first <= last_pos,
        return_work,
    )
    grad_kv_own = lax.psum_scatter(
        grad_kv.astype(jnp.bfloat16), "seq", scatter_dimension=0, tiled=True
    ).astype(jnp.float32)
    grad_query_rows = jnp.transpose(grad_query, (1, 0, 2)).reshape(rows, width)
    grad_projected = jnp.concatenate([grad_query_rows, grad_kv_own], axis=1).astype(jnp.bfloat16)
    grad_w_qkv = jnp.dot(hidden_one.T, grad_projected, preferred_element_type=jnp.float32)
    grad_proj_wide = grad_projected.astype(jnp.float32)
    grad_b_query = jnp.sum(grad_proj_wide[:, :width], axis=0)
    grad_b_value = jnp.sum(grad_proj_wide[:, 2 * width :], axis=0)
    grad_hidden_one = jnp.dot(grad_projected, w_qkv.T, preferred_element_type=jnp.float32)
    grad_in_norm, grad_gain_one, grad_shift_one = back_one(grad_hidden_one)
    grad_inputs = grad_middle + grad_in_norm
    summed = lax.psum(
        (
            grad_gain_one,
            grad_shift_one,
            grad_w_qkv,
            grad_b_query,
            grad_b_value,
            grad_w_out,
            grad_b_out,
            grad_gain_two,
            grad_shift_two,
            grad_w_up,
            grad_b_up,
            grad_w_down,
            grad_b_down,
        ),
        ("seq", "batch"),
    )
    return (
        result.astype(jnp.bfloat16)[None],
        grad_inputs[None],
        summed[0],
        summed[1],
        summed[2],
        summed[3],
        summed[4],
        summed[5],
        summed[6],
        summed[7],
        summed[8],
        summed[9],
        summed[10],
        summed[11],
        summed[12],
    )


def solution(mesh):
    return jax.shard_map(
        shards,
        mesh=mesh,
        in_specs=(
            P("batch", "seq", None),
            P("batch", "seq", None),
            P(),
            P(),
            P(),
            P(),
            P(),
            P(),
            P(),
            P(),
            P(),
            P(),
            P(),
            P(),
            P(),
        ),
        out_specs=(
            P("batch", "seq", None),
            P("batch", "seq", None),
            P(),
            P(),
            P(),
            P(),
            P(),
            P(),
            P(),
            P(),
            P(),
            P(),
            P(),
            P(),
            P(),
        ),
        check_vma=False,
    )
```

profile of v0, /device:TPU:10, one launch (start us, length us, event | category | flops | bytes accessed | tf_op | source)
XLA Modules:
  0.0 1080.5 jit_solution(7248955041994857887)
XLA Ops:
  11.1 2.2 fusion.32
  15.3 1.8 slice.37
  17.1 1.9 copy.43
  19.5 87.8 %all-gather.2.cloned.1.call-done = bf16[4096,1536]{1,0:T(8,128)(2,1)} async-done(((bf16[256,1536]{1,0:T(8,128)(2,1)}), bf16[4096,1536]{1,0:T(8,128)(2,1)}) %all-gather.2.cloned.1.call-update) | async-done | bytes 12582928 | tf_op jit(solution)/shard_map/all_gather | solution.py:114
  107.3 16.6 %copy.44 = bf16[16,256,1536]{1,2,0:T(8,128)(2,1)} copy(bf16[16,256,1536]{2,1,0:T(8,128)(2,1)} %bitcast.150) | data formatting | bytes 25165824
  125.5 70.6 %while.28 = (s32[]{:T(128)}, f32[12,256]{1,0:T(8,128)S(1)}, f32[12,256]{1,0:T(8,128)}, f32[12,256,64]{1,2,0:T(8,128)}, s32[16]{0:T(128)}, /*index=5*/s32[]{:T(12...) while((s32[]{:T(128)}, f32[12,256]{1,0:T(8,128)S(1)}, ...), condition=%wide.region_7.8_spmd.clone, body=%wide.region_2.7_spmd.clone.sunk | while | flops 212015616 | bytes 23764392 | solution.py:53
  128.0 6.3 conditional.6
  128.0 1.5 broadcast_add_fusion
  136.7 6.2 conditional.6
  136.7 1.5 broadcast_add_fusion
  145.4 6.2 conditional.6
  145.4 1.5 broadcast_add_fusion
  154.1 6.3 conditional.6
  154.1 1.5 broadcast_add_fusion
  162.8 6.2 conditional.6
  162.8 1.5 broadcast_add_fusion
  197.5 2.4 fusion.80
  200.9 1.5 convolution_add_fusion.1
  202.4 3.7 convert_reduce_fusion
  206.2 2.2 multiply_reduce_fusion
  212.5 1.9 copy.45
  214.4 2.0 fusion.56
  217.3 11.5 %broadcast_in_dim.99 = f32[4096,1536]{0,1:T(8,128)} broadcast(f32[]{:T(128)} %constant.80.clone.1), dimensions={} | broadcast | bytes 25165828 | tf_op jit(solution)/shard_map/broadcast_in_dim | solution.py:186
  228.9 130.7 %while.29 = (s32[]{:T(128)}, f32[12,256,64]{1,2,0:T(8,128)}, f32[4096,1536]{0,1:T(8,128)}, s32[16]{0:T(128)S(1)}, s32[]{:T(128)}, /*index=5*/bf16[16,256,1536]{1...) while((s32[]{:T(128)}, f32[12,256,64]{1,2,0:T(8,128)}, ...), condition=%wide.region_15.16_spmd.clone, body=%wide.region_12.15_spmd.clone.sunk | while | flops 514195968 | bytes 40840696 | solution.py:53
  230.0 22.4 %conditional.7 = ((f32[12,256,64]{1,2,0:T(8,128)}, f32[4096,1536]{0,1:T(8,128)})) conditional(s32[]{:T(128)} %convert_element_type.165, (f32[12,256,64]{1,2,0:T(8,128)}, f32[4096,1536]{0,1:T(8,128)}) %tuple.93, (s32[]{:T(128)}, s32[256]{0:T(256)S(1)}, s32[]{:T(128)}, bf16[16,256,1536]{1,2,0:T(8,128)(2,1)}, s32[]{:T(128)}, ...), branch_computations={%region_13.13_spmd, %region_14.14_spmd} | conditional | flops 514195968 | bytes 40839412 | solution.py:47
  235.2 1.7 fusion.25
  237.0 1.5 convolution_multiply_fusion.1
  240.1 3.8 maximum_add_fusion
  243.8 8.6 dynamic_update_slice.3
  253.5 22.5 %conditional.7 = ((f32[12,256,64]{1,2,0:T(8,128)}, f32[4096,1536]{0,1:T(8,128)})) conditional(s32[]{:T(128)} %convert_element_type.165, (f32[12,256,64]{1,2,0:T(8,128)}, f32[4096,1536]{0,1:T(8,128)}) %tuple.93, (s32[]{:T(128)}, s32[256]{0:T(256)S(1)}, s32[]{:T(128)}, bf16[16,256,1536]{1,2,0:T(8,128)(2,1)}, s32[]{:T(128)}, ...), branch_computations={%region_13.13_spmd, %region_14.14_spmd} | conditional | flops 514195968 | bytes 40839412 | solution.py:47
  258.8 1.7 fusion.25
  260.5 1.5 convolution_multiply_fusion.1
  263.6 3.8 maximum_add_fusion
  267.4 8.6 dynamic_update_slice.3
  277.1 22.5 %conditional.7 = ((f32[12,256,64]{1,2,0:T(8,128)}, f32[4096,1536]{0,1:T(8,128)})) conditional(s32[]{:T(128)} %convert_element_type.165, (f32[12,256,64]{1,2,0:T(8,128)}, f32[4096,1536]{0,1:T(8,128)}) %tuple.93, (s32[]{:T(128)}, s32[256]{0:T(256)S(1)}, s32[]{:T(128)}, bf16[16,256,1536]{1,2,0:T(8,128)(2,1)}, s32[]{:T(128)}, ...), branch_computations={%region_13.13_spmd, %region_14.14_spmd} | conditional | flops 514195968 | bytes 40839412 | solution.py:47
  282.4 1.7 fusion.25
  284.1 1.5 convolution_multiply_fusion.1
  287.2 3.8 maximum_add_fusion
  291.0 8.7 dynamic_update_slice.3
  300.8 22.5 %conditional.7 = ((f32[12,256,64]{1,2,0:T(8,128)}, f32[4096,1536]{0,1:T(8,128)})) conditional(s32[]{:T(128)} %convert_element_type.165, (f32[12,256,64]{1,2,0:T(8,128)}, f32[4096,1536]{0,1:T(8,128)}) %tuple.93, (s32[]{:T(128)}, s32[256]{0:T(256)S(1)}, s32[]{:T(128)}, bf16[16,256,1536]{1,2,0:T(8,128)(2,1)}, s32[]{:T(128)}, ...), branch_computations={%region_13.13_spmd, %region_14.14_spmd} | conditional | flops 514195968 | bytes 40839412 | solution.py:47
  306.0 1.7 fusion.25
  307.7 1.5 convolution_multiply_fusion.1
  310.9 3.8 maximum_add_fusion
  314.6 8.6 dynamic_update_slice.3
  324.4 22.5 %conditional.7 = ((f32[12,256,64]{1,2,0:T(8,128)}, f32[4096,1536]{0,1:T(8,128)})) conditional(s32[]{:T(128)} %convert_element_type.165, (f32[12,256,64]{1,2,0:T(8,128)}, f32[4096,1536]{0,1:T(8,128)}) %tuple.93, (s32[]{:T(128)}, s32[256]{0:T(256)S(1)}, s32[]{:T(128)}, bf16[16,256,1536]{1,2,0:T(8,128)(2,1)}, s32[]{:T(128)}, ...), branch_computations={%region_13.13_spmd, %region_14.14_spmd} | conditional | flops 514195968 | bytes 40839412 | solution.py:47
  329.6 1.7 fusion.25
  331.3 1.5 convolution_multiply_fusion.1
  334.5 3.8 maximum_add_fusion
  338.2 8.6 dynamic_update_slice.3
  359.5 13.2 %convert_element_type.85 = bf16[4096,1536]{0,1:T(8,128)(2,1)} convert(f32[4096,1536]{0,1:T(8,128)} %get-tuple-element.257) | non-fusion elementwise | flops 6291456 | bytes 37748736 | tf_op jit(solution)/shard_map/convert_element_type | solution.py:196
  372.9 2.1 convert.6
  375.0 3.0 fusion.82
  378.1 5.3 fusion.74
  383.5 6.0 fusion.58
  389.4 418.2 %reduce-scatter.2.cloned.1.call-done = bf16[256,1536]{0,1:T(8,128)(2,1)} async-done(((bf16[4096,1536]{0,1:T(8,128)(2,1)}), bf16[256,1536]{0,1:T(8,128)(2,1)}) %reduce-scatter.2.cloned.1.call-update) | async-done | bytes 786448 | tf_op jit(solution)/shard_map/reduce_scatter | solution.py:195
  807.6 5.6 fusion.65
  813.9 6.2 fusion.43
  821.2 1.8 fusion.75
  824.1 1.9 convert_reduce_fusion.1
  825.9 64.7 %all-reduce = (f32[768]{0:T(1024)}, f32[768]{0:T(1024)}, f32[768]{0:T(1024)}, f32[768]{0:T(1024)}, f32[768]{0:T(1024)}, /*index=5*/f32[768]{0:T(1024)}, f32[768]{0:T(1024)}, f32[3072]{0:T(1024)}, f32[768]{0:T(1024)}) all-reduce(f32[768]{0:T(1024)} %get-tuple-element.361, ...), channel_id=1, replica_groups=mesh['seq'=16,'batch'=8] {'seq','batch'}, use_global_device_ids=true, to_apply=%region_20.21 | all-reduce | flops 9216 | bytes 73728 | tf_op jit(solution)/shard_map/psum | solution.py:207
  890.6 162.2 %all-reduce.4.cloned.1.call-done = (f32[768,2304]{1,0:T(8,128)}, f32[768,768]{1,0:T(8,128)}, f32[768,3072]{1,0:T(8,128)}, f32[3072,768]{1,0:T(8,128)}) async-done(((f32[768,2304]{1,0:T(8,128)}, f32[768,768]{1,0:T(8,128)}, f32[768,3072]{1,0:T(8,128)}, f32[3072,768]{1,0:T(8,128)}), (f32[768,2304]{1,0:T(8,128)}, f32[768,768]{1,0:T(8,128)}, f32[768,3072]{1,0:T(8,128)}, ...) | async-done | bytes 28311568 | tf_op jit(solution)/shard_map/psum | solution.py:207
  1052.9 6.6 copy.98
  1060.9 9.3 copy.100
  1070.2 3.7 copy.101
  (412 shorter events, 106.1 us)
Async XLA Ops:
  7.2 3.9 copy-start
  7.2 100.1 %all-gather.2.cloned.1.call-start = ((), (), s32[]{:S(2)}) async-start(), calls=%async_computation.1 | async-start | bytes 13369344 | tf_op jit(solution)/shard_map/all_gather | solution.py:114
  8.5 4.7 copy-start.37
  9.8 3.5 copy-start.39
  15.2 792.4 %reduce-scatter.2.cloned.1.call-start = ((), (), s32[]{:S(2)}) async-start(), calls=%async_computation.2 | async-start | bytes 13369344 | tf_op jit(solution)/shard_map/reduce_scatter | solution.py:195
  128.0 2.8 copy-start.1
  130.8 1.5 copy-start.26
  130.8 1.5 copy-start.8
  136.7 2.8 copy-start.1
  139.5 1.5 copy-start.26
  139.6 1.5 copy-start.8
  145.4 2.8 copy-start.1
  148.2 1.5 copy-start.26
  148.3 1.5 copy-start.8
  154.1 2.8 copy-start.1
  156.9 1.5 copy-start.26
  157.0 1.5 copy-start.8
  162.8 2.8 copy-start.1
  165.7 1.5 copy-start.26
  165.7 1.5 copy-start.8
  196.1 4.1 copy-start.28
  196.1 4.8 copy-start.32
  196.1 4.8 copy-start.34
  196.1 4.8 copy-start.52
  196.1 4.8 copy-start.53
  197.5 2.7 copy-start.15
  197.5 4.9 slice-start.3
  200.0 8.4 copy-start.6
  200.0 8.4 copy-start.41
  200.2 8.2 copy-start.46
  200.9 1.5 copy-start.18
  200.9 1.5 slice-start.4
  202.4 3.7 copy-start.12
  206.2 2.2 copy-start.24
  208.4 2.9 copy-start.14
  208.4 6.0 copy-start.29
  208.8 1.7 copy-start.50
  217.3 11.5 %copy-start.55 = (s32[16]{0:T(128)S(1)}, s32[16]{0:T(128)}, u32[]{:S(2)}) copy-start(s32[16]{0:T(128)} %get-tuple-element.701) | copy-start | bytes 196
  254.8 1.4 copy-start.23
  254.8 1.4 copy-start.43
  372.8 5.2 copy-start.33
  372.8 5.2 copy-start.35
  372.8 5.2 copy-start.42
  372.9 5.2 copy-start.47
  372.9 680.0 %all-reduce.4.cloned.1.call-start = ((), (), s32[]{:S(2)}) async-start(), calls=%async_computation.3 | async-start | bytes 56623104 | tf_op jit(solution)/shard_map/psum | solution.py:207
  372.9 5.1 copy-start.7
  372.9 5.1 copy-start.25
  378.1 5.4 copy-start.13
  378.1 5.3 copy-start.19
  383.4 424.2 %copy-start.31 = (f32[768]{0:T(1024)S(1)}, f32[768]{0:T(1024)}, u32[]{:S(2)}) copy-start(f32[768]{0:T(1024)} %param.25) | copy-start | bytes 9220
  383.4 424.2 %copy-start.36 = (f32[768]{0:T(1024)S(1)}, f32[768]{0:T(1024)}, u32[]{:S(2)}) copy-start(f32[768]{0:T(1024)} %param.26) | copy-start | bytes 9220
  383.4 424.2 %copy-start.38 = (f32[256]{0:T(256)S(1)}, f32[256]{0:T(256)}, u32[]{:S(2)}) copy-start(f32[256]{0:T(256)} %copy-done.37) | copy-start | bytes 3076
  383.5 424.2 %copy-start.40 = (f32[256]{0:T(256)S(1)}, f32[256]{0:T(256)}, u32[]{:S(2)}) copy-start(f32[256]{0:T(256)} %copy-done.39) | copy-start | bytes 3076
  813.9 6.2 copy-start.17
  813.9 6.2 copy-start.21
  821.2 1.8 copy-start.49
  821.2 2.8 copy-start.11
  821.2 2.8 copy-start.20
  821.2 2.8 copy-start.51
  823.0 2.9 copy-start.44
  1052.9 6.6 copy-start.22
  1059.4 10.7 slice-start
  1060.8 9.3 slice-start.1
  1060.9 9.3 slice-start.2
  (44 other events, 49.9 us)
Sparse Core Ops, SparseCore 0:
  15.4 91.9 all-gather.1
  372.9 434.6 reduce-scatter.1
  816.1 236.6 all-reduce.3
where the time goes:
time: 1090 us; the launch traced here: 1080 us
  waiting for transfers between devices  668 us (61%)
  local copies, waits for them, and re-layouts  165 us (15%)
  matrix products  76.7 us (7%)
  blocking collectives  64.7 us (6%)
  other arithmetic  62.1 us (6%)
  loops' own time  29.5 us (3%)
  between operations  14.3 us (1%)
    reduce_scatter x1, waiting for transfers between devices, shards(): lax.psum_scatter(grad_kv.astype(jnp.bfloat16), 'seq', scatter_dimension=0...  418 us
    psum x1, waiting for transfers between devices, shards(): lax.psum((grad_gain_one, grad_shift_one, grad_w_qkv, grad_b_query, grad_b...  162 us
    all_gather x1, waiting for transfers between devices, shards(): lax.all_gather(keys_values, 'seq', axis=0, tiled=True)  87.8 us
    psum x1, blocking collectives, shards(): lax.psum((grad_gain_one, grad_shift_one, grad_w_qkv, grad_b_query, grad_b...  64.7 us
    dynamic_update_slice x5, local copies, waits for them, and re-layouts, return_work(): lax.dynamic_update_slice_in_dim(grad_kv, current + update, first, 0)  43.1 us
    unnamed x105, local copies, waits for them, and re-layouts  41.7 us
    dynamic_slice x32, local copies, waits for them, and re-layouts, over_blocks(): result, _ = lax.scan(step, carry, (blocks, firsts))  28.6 us
  transfers between devices with their start and end apart: 3, of which 3 were waited for; matrix products, arithmetic and copies ran while one was open for 3% of the time, Pallas kernels for 0%

commit v1 on v0

v1 whole, which is shorter than its diff:
```python
import jax
import jax.numpy as jnp
from jax import lax
from jax.experimental import pallas as pl
from jax.experimental.pallas import tpu as pltpu
from jax.sharding import PartitionSpec as P

H = 12
HD = 64
LOG2E = 1.4426950408889634
BF = jnp.bfloat16
F32 = jnp.float32


def shift_pairs(axis, step):
    pairs = []
    for s in range(16):
        for b in range(8):
            y, z, c, x = s // 4, (s // 2 % 2) * 2 + b // 4, s % 2, b % 4
            if axis == "y":
                y = (y + step) % 4
            elif axis == "z":
                z = (z + step) % 4
            elif axis == "x":
                x = (x + step) % 4
            else:
                c = c ^ step
            source = (y * 4 + (z // 2) * 2 + c) * 8 + (z % 2) * 4 + x
            pairs.append((source, s * 8 + b))
    return pairs


def fetch(array, axis, step):
    return lax.ppermute(array, ("seq", "batch"), shift_pairs(axis, step))


def reduce_scatter(array, axis, index):
    count = array.shape[0]
    total = lax.dynamic_index_in_dim(array, index, 0, keepdims=False).astype(F32)
    for step in range(1, count):
        target = lax.rem(index + step, count)
        piece = lax.dynamic_index_in_dim(array, target, 0, keepdims=False)
        total = total + fetch(piece, axis, count - step).astype(F32)
    return total.astype(array.dtype)


def all_gather(array, axis, index, count):
    pieces = [array] + [fetch(array, axis, step) for step in range(1, count)]
    return roll_slots(pieces, index)


def roll_slots(pieces, index):
    count = len(pieces)
    stacked = jnp.stack(pieces + pieces[:-1])
    return lax.dynamic_slice_in_dim(stacked, lax.rem(count - index, count), count, 0)


def sum_all(vector):
    vector = vector + fetch(vector, "c", 1)
    for axis in ("y", "z", "x"):
        vector = (vector + fetch(vector, axis, 2)) + (fetch(vector, axis, 1) + fetch(vector, axis, 3))
    return vector


def nt(left, right):
    return lax.dot_general(left, right, (((1,), (1,)), ((), ())), preferred_element_type=F32)


def fwd_kernel(slot_of, block_of, q_ref, kv_ref, kvt_ref, o_ref, o32_ref, lse_ref, m_ref, l_ref, acc_ref):
    me = pl.program_id(0)
    count = block_of[me]
    m_ref[...] = jnp.full(m_ref.shape, -1e30, F32)
    l_ref[...] = jnp.zeros(l_ref.shape, F32)
    acc_ref[...] = jnp.zeros(acc_ref.shape, F32)

    def step(slot, masked):
        for h in range(3):
            q = q_ref[0, :, h * HD : (h + 1) * HD]
            k = kv_ref[slot, :, h * 128 : h * 128 + HD]
            s = nt(k, q) * LOG2E
            if masked:
                keys = lax.broadcasted_iota(jnp.int32, s.shape, 0)
                queries = lax.broadcasted_iota(jnp.int32, s.shape, 1)
                s = jnp.where(keys <= queries, s, -1e30)
            old = m_ref[h]
            new = jnp.maximum(old, jnp.max(s, axis=0, keepdims=True))
            p = jnp.exp2(s - new)
            factor = jnp.exp2(old - new)
            m_ref[h] = new
            l_ref[h] = l_ref[h] * factor + jnp.sum(p, axis=0, keepdims=True)
            vt = kvt_ref[slot, h * 128 + HD : (h + 1) * 128, :]
            acc_ref[h] = acc_ref[h] * factor + jnp.dot(vt, p.astype(BF), preferred_element_type=F32)

    step(me * 4, True)

    def body(b, carry):
        step(slot_of[b], False)
        return carry

    lax.fori_loop(0, count, body, 0)
    for h in range(3):
        o = (acc_ref[h] / l_ref[h]).T
        o32_ref[0, :, h * HD : (h + 1) * HD] = o
        o_ref[0, :, h * HD : (h + 1) * HD] = o.astype(BF)
        lse_ref[0, h : h + 1, :] = m_ref[h] + jnp.log2(l_ref[h])


def bwd_kernel(slot_of, block_of, q_ref, do_ref, o32_ref, lse_ref, kv_ref, kvt_ref, dq_ref, dkv_ref, qdo_ref, delta_ref, dqt_ref):
    me = pl.program_id(0)
    count = block_of[me]

    @pl.when(me == 0)
    def _():
        dkv_ref[...] = jnp.zeros(dkv_ref.shape, F32)

    zero = jnp.zeros((256, HD), BF)
    for h in range(3):
        do = do_ref[0, :, h * HD : (h + 1) * HD]
        qdo_ref[h, :256, :] = jnp.concatenate([q_ref[0, :, h * HD : (h + 1) * HD], zero], axis=1)
        qdo_ref[h, 256:, :] = jnp.concatenate([zero, do], axis=1)
        prod = do.astype(F32) * o32_ref[0, :, h * HD : (h + 1) * HD]
        delta_ref[h] = jnp.sum(prod.T, axis=0, keepdims=True)
    dqt_ref[...] = jnp.zeros(dqt_ref.shape, F32)

    def step(slot, masked):
        for h in range(3):
            qdo = qdo_ref[h]
            both = nt(kv_ref[slot, :, h * 128 : (h + 1) * 128], qdo)
            s = both[:, :256] * LOG2E - lse_ref[0, h : h + 1, :]
            p = jnp.exp2(s)
            if masked:
                keys = lax.broadcasted_iota(jnp.int32, s.shape, 0)
                queries = lax.broadcasted_iota(jnp.int32, s.shape, 1)
                p = jnp.where(keys <= queries, p, 0.0)
            ds = (p * (both[:, 256:] - delta_ref[h])).astype(BF)
            w = jnp.concatenate([ds, p.astype(BF)], axis=1)
            dkv_ref[slot, :, h * 128 : (h + 1) * 128] += jnp.dot(w, qdo, preferred_element_type=F32)
            kt = kvt_ref[slot, h * 128 : h * 128 + HD, :]
            dqt_ref[h] += jnp.dot(kt, ds, preferred_element_type=F32)

    step(me * 4, True)

    def body(b, carry):
        step(slot_of[b], False)
        return carry

    lax.fori_loop(0, count, body, 0)
    for h in range(3):
        dq_ref[0, :, h * HD : (h + 1) * HD] = (dqt_ref[h].T * 0.125).astype(BF)


def whole(shape):
    return pl.BlockSpec(shape, lambda i, *_: (0,) * len(shape))


def of_slot(shape):
    return pl.BlockSpec((1,) + shape, lambda i, *_: (i,) + (0,) * len(shape))


def attend(slot_of, block_of, q, kv, kvt):
    return pl.pallas_call(
        fwd_kernel,
        grid_spec=pltpu.PrefetchScalarGridSpec(
            num_scalar_prefetch=2,
            grid=(4,),
            in_specs=[of_slot((256, 192)), whole((16, 256, 384)), whole((16, 384, 256))],
            out_specs=[of_slot((256, 192)), of_slot((256, 192)), of_slot((3, 256))],
            scratch_shapes=[
                pltpu.VMEM((3, 1, 256), F32),
                pltpu.VMEM((3, 1, 256), F32),
                pltpu.VMEM((3, HD, 256), F32),
            ],
        ),
        out_shape=[
            jax.ShapeDtypeStruct((4, 256, 192), BF),
            jax.ShapeDtypeStruct((4, 256, 192), F32),
            jax.ShapeDtypeStruct((4, 3, 256), F32),
        ],
        compiler_params=pltpu.CompilerParams(vmem_limit_bytes=48 * 2**20),
        name="attend",
    )(slot_of, block_of, q, kv, kvt)


def attend_back(slot_of, block_of, q, do, o32, lse, kv, kvt):
    return pl.pallas_call(
        bwd_kernel,
        grid_spec=pltpu.PrefetchScalarGridSpec(
            num_scalar_prefetch=2,
            grid=(4,),
            in_specs=[
                of_slot((256, 192)),
                of_slot((256, 192)),
                of_slot((256, 192)),
                of_slot((3, 256)),
                whole((16, 256, 384)),
                whole((16, 384, 256)),
            ],
            out_specs=[of_slot((256, 192)), whole((16, 256, 384))],
            scratch_shapes=[
                pltpu.VMEM((3, 512, 128), BF),
                pltpu.VMEM((3, 1, 256), F32),
                pltpu.VMEM((3, HD, 256), F32),
            ],
        ),
        out_shape=[
            jax.ShapeDtypeStruct((4, 256, 192), BF),
            jax.ShapeDtypeStruct((16, 256, 384), F32),
        ],
        compiler_params=pltpu.CompilerParams(vmem_limit_bytes=56 * 2**20),
        name="attend_back",
    )(slot_of, block_of, q, do, o32, lse, kv, kvt)


def layer_norm(values, gain, shift):
    center = values - jnp.mean(values, axis=-1, keepdims=True)
    spread = jnp.mean(center * center, axis=-1, keepdims=True)
    return center * lax.rsqrt(spread + 1e-05) * gain + shift


def shards(
    tokens,
    cotangent,
    ln1_gain,
    ln1_shift,
    w_qkv,
    b_query,
    b_value,
    w_out,
    b_out,
    ln2_gain,
    ln2_shift,
    w_up,
    b_up,
    w_down,
    b_down,
):
    seq, batch = lax.axis_index("seq"), lax.axis_index("batch")
    y, zh, c = seq // 4, lax.rem(seq // 2, 2), lax.rem(seq, 2)
    z, x = zh * 2 + batch // 4, lax.rem(batch, 4)

    inputs = tokens[0].astype(F32)
    normed_one, back_one = jax.vjp(layer_norm, inputs, ln1_gain, ln1_shift)
    h1 = normed_one.astype(BF)

    held = {(0, 0): h1}
    for dy in (1, 2, 3):
        held[dy, 0] = fetch(h1, "y", dy)
    held[0, 1] = fetch(h1, "z", 2)
    held[2, 1] = fetch(held[0, 1], "y", 2)
    for dy in (1, 3):
        held[dy, 1] = fetch(held[dy, 0], "z", 2)
    order = [(dy, dz) for dy in range(4) for dz in range(2)]
    mine = jnp.stack([held[p] for p in order])
    other = fetch(mine, "c", 1)
    h1_all = jnp.stack([mine, other], axis=1).reshape(16, 256, 768)

    dy, dz, dc = jnp.meshgrid(jnp.arange(4), jnp.arange(2), jnp.arange(2), indexing="ij")
    blocks = (lax.rem(y + dy, 4) * 4 + (zh ^ dz) * 2 + (c ^ dc)).reshape(16).astype(jnp.int32)
    slot_of = jnp.zeros((16,), jnp.int32).at[blocks].set(jnp.arange(16, dtype=jnp.int32))
    block_of = blocks[::4]

    w_group = lax.dynamic_slice_in_dim(w_qkv.reshape(768, 3, 768), y * 192, 192, 2)
    bq_group = lax.dynamic_slice_in_dim(b_query, y * 192, 192, 0)
    bv_group = lax.dynamic_slice_in_dim(b_value, y * 192, 192, 0)
    w_kv = jnp.stack([w_group[:, 1].reshape(768, 3, HD), w_group[:, 2].reshape(768, 3, HD)], axis=2).reshape(768, 384)
    b_kv = jnp.stack([jnp.zeros((3, HD), F32), bv_group.reshape(3, HD)], axis=1).reshape(384)
    kv = (jnp.einsum("btf,fc->btc", h1_all, w_kv, preferred_element_type=F32) + b_kv).astype(BF)
    kvt = jnp.swapaxes(kv, 1, 2)
    h1_query = h1_all[::4]
    q = jnp.einsum("btf,fc->btc", h1_query, w_group[:, 0], preferred_element_type=F32) + bq_group
    q = q.astype(BF) * jnp.asarray(0.125, BF)

    o, o32, lse = attend(slot_of, block_of, q, kv, kvt)

    heads = [o[0]] + [fetch(o[4 - e], "y", e) for e in (1, 2, 3)]
    attended = roll_slots(heads, y).transpose(1, 0, 2).reshape(256, 768)

    middle = inputs + jnp.dot(attended, w_out, preferred_element_type=F32) + b_out
    normed_two, back_two = jax.vjp(layer_norm, middle, ln2_gain, ln2_shift)
    h2 = normed_two.astype(BF)
    inner = jnp.dot(h2, w_up, preferred_element_type=F32) + b_up
    activated, back_gelu = jax.vjp(lambda value: jax.nn.gelu(value, approximate=True), inner)
    g = activated.astype(BF)
    result = middle + jnp.dot(g, w_down, preferred_element_type=F32) + b_down
    dy_low = cotangent[0]
    seed = dy_low.astype(F32)
    grad_b_down = jnp.sum(seed, axis=0)
    grad_act = jnp.dot(dy_low, w_down.T, preferred_element_type=F32)
    du = back_gelu(grad_act)[0].astype(BF)
    grad_b_up = jnp.sum(du.astype(F32), axis=0)
    grad_h2 = jnp.dot(du, w_up.T, preferred_element_type=F32)
    grad_mid_norm, grad_gain_two, grad_shift_two = back_two(grad_h2)
    grad_middle = seed + grad_mid_norm
    da = grad_middle.astype(BF)
    grad_b_out = jnp.sum(da.astype(F32), axis=0)
    do = jnp.dot(da, w_out.T, preferred_element_type=F32).astype(BF)

    do_groups = do.reshape(256, 4, 192).transpose(1, 0, 2)
    do_mine = [lax.dynamic_index_in_dim(do_groups, y, 0, keepdims=False)]
    for e in (1, 2, 3):
        piece = lax.dynamic_index_in_dim(do_groups, lax.rem(y + 4 - e, 4), 0, keepdims=False)
        do_mine.append(fetch(piece, "y", e))
    do_mine = jnp.stack(do_mine)

    def halves(array):
        parts = array.reshape(256, 2, -1)
        own = lax.dynamic_index_in_dim(parts, c, 1, keepdims=False)
        return jnp.concatenate([own, fetch(lax.dynamic_index_in_dim(parts, 1 - c, 1, keepdims=False), "c", 1)])

    def pair(array):
        return jnp.concatenate([array, fetch(array, "c", 1)])

    def tn(left, right):
        return lax.dot_general(left, right, (((0,), (0,)), ((), ())), preferred_element_type=F32)

    gw_down = tn(halves(g), pair(dy_low)).astype(BF)
    gw_up = tn(halves(du), pair(h2)).astype(BF)
    gw_out = tn(halves(attended), pair(da)).astype(BF)

    places = {"x": x, "y": y, "z": z}

    def sum_weights(array, axes):
        shape = array.shape
        for axis in axes:
            array = reduce_scatter(array.reshape(4, -1, 768), axis, places[axis])
        for axis in reversed(axes):
            array = all_gather(array, axis, places[axis], 4).reshape(-1, 768)
        return array

    def join_cores(array):
        return all_gather(array, "c", c, 2).reshape(-1, 768)

    gw_down = join_cores(sum_weights(gw_down, ("x", "y", "z"))).astype(F32)
    gw_up = join_cores(sum_weights(gw_up, ("z", "x", "y"))).T.astype(F32)
    gw_out = join_cores(sum_weights(gw_out, ("y", "x", "z"))).astype(F32)

    dq, dkv32 = attend_back(slot_of, block_of, q, do_mine, o32, lse, kv, kvt)
    dkv = dkv32.astype(BF)

    gq = tn(dq.reshape(1024, 192), h1_query.reshape(1024, 768))
    gkv = tn(dkv.reshape(4096, 384), h1_all.reshape(4096, 768))
    gkv = gkv.reshape(3, 2, HD, 768)
    gw = jnp.concatenate([gq, gkv[:, 0].reshape(192, 768), gkv[:, 1].reshape(192, 768)]).astype(BF)
    gw = reduce_scatter(gw.reshape(2, 288, 768), "c", c)
    gw = reduce_scatter(gw.reshape(4, 72, 768), "x", x)
    gw = reduce_scatter(jnp.pad(gw, ((0, 24), (0, 0))).reshape(4, 24, 768), "z", z)
    gw = all_gather(gw, "z", z, 4).reshape(96, 768)[:72]
    gw = all_gather(gw, "x", x, 4).reshape(288, 768)
    gw = all_gather(gw, "c", c, 2).reshape(576, 768)
    gw = all_gather(gw, "y", y, 4).reshape(4, 3, 192, 768)
    gw_qkv = gw.transpose(1, 0, 2, 3).reshape(2304, 768).T.astype(F32)

    parts = dkv.reshape(4, 2, 2, 256, 384)
    parts = parts[:, :, 0].astype(F32) + fetch(parts[:, :, 1], "c", 1).astype(F32)
    parts = parts.astype(BF)
    parts = parts[:, 0].astype(F32) + fetch(parts[:, 1], "z", 2).astype(F32)
    parts = parts.astype(BF)
    parts = jnp.concatenate([dq, parts], axis=2)
    groups = [parts[0]] + [fetch(parts[4 - e], "y", e) for e in (1, 2, 3)]
    groups = roll_slots(groups, y)
    dq_rows = groups[:, :, :192].transpose(1, 0, 2).reshape(256, 768)
    dkv_rows = groups[:, :, 192:].reshape(4, 256, 3, 2, HD).transpose(1, 3, 0, 2, 4).reshape(256, 2, 768)
    dk_rows = dkv_rows[:, 0]
    dv_rows = dkv_rows[:, 1]
    dqkv = jnp.concatenate([dq_rows, dk_rows, dv_rows], axis=1)
    grad_b_query = jnp.sum(dq_rows.astype(F32), axis=0)
    grad_b_value = jnp.sum(dv_rows.astype(F32), axis=0)
    grad_h1 = jnp.dot(dqkv, w_qkv.T, preferred_element_type=F32)
    grad_in_norm, grad_gain_one, grad_shift_one = back_one(grad_h1)
    grad_inputs = grad_middle + grad_in_norm

    small = jnp.stack([grad_gain_one, grad_shift_one, grad_b_query, grad_b_value, grad_b_out, grad_gain_two, grad_shift_two, grad_b_down])
    small = jnp.concatenate([small, grad_b_up.reshape(4, 768)])
    small = sum_all(small)
    return (
        result.astype(BF)[None],
        grad_inputs[None],
        small[0],
        small[1],
        gw_qkv,
        small[2],
        small[3],
        gw_out,
        small[4],
        small[5],
        small[6],
        gw_up,
        small[8:12].reshape(3072),
        gw_down,
        small[7],
    )


def solution(mesh):
    split = P("batch", "seq", None)
    return jax.shard_map(
        shards,
        mesh=mesh,
        in_specs=(split, split) + (P(),) * 13,
        out_specs=(split, split) + (P(),) * 13,
        check_vma=False,
    )
```

time: 1090 us -> 613 us (0.56)
  waiting for transfers between devices: 668 us -> 126 us
  starting transfers between devices: 0.12 us -> 193 us
  blocking collectives: 64.7 us -> 0 us
  Pallas kernels: 0 us -> 61.8 us
  matrix products: 76.7 us -> 40.1 us
  local copies, waits for them, and re-layouts: 165 us -> 129 us
  loops' own time: 29.5 us -> 0 us
  between operations: 14.3 us -> 2.88 us
  other arithmetic: 62.1 us -> 50.7 us
    reduce_scatter x1 -> x0, waiting for transfers between devices: 418 us -> none  [shards(): lax.psum_scatter(grad_kv.astype(jnp.bfloat16), 'seq', scatter_dimension=0...]
    ppermute x0 -> x109, starting transfers between devices: none -> 193 us  [fetch(): return lax.ppermute(array, ('seq', 'batch'), shift_pairs(axis, step))]
    psum x1 -> x0, waiting for transfers between devices: 162 us -> none  [shards(): lax.psum((grad_gain_one, grad_shift_one, grad_w_qkv, grad_b_query, grad_b...]
    ppermute x0 -> x109, waiting for transfers between devices: none -> 126 us  [fetch(): return lax.ppermute(array, ('seq', 'batch'), shift_pairs(axis, step))]
    all_gather x1 -> x0, waiting for transfers between devices: 87.8 us -> none  [shards(): lax.all_gather(keys_values, 'seq', axis=0, tiled=True)]
    psum x1 -> x0, blocking collectives: 64.7 us -> none  [shards(): lax.psum((grad_gain_one, grad_shift_one, grad_w_qkv, grad_b_query, grad_b...]
    pallas_call x0 -> x2, Pallas kernels: none -> 61.8 us  [the longest x1 31.9 us: attend_back(): pl.pallas_call(bwd_kernel, grid_spec=pltpu.PrefetchScalarGridSpec(num_sca...]
    dynamic_update_slice x5 -> x0, local copies, waits for them, and re-layouts: 43.1 us -> none  [return_work(): lax.dynamic_update_slice_in_dim(grad_kv, current + update, first, 0)]
  transfers between devices with their start and end apart: 3 -> 109, of which waited for: 3 -> 46; matrix products, arithmetic and copies ran while one was open for 3% -> 30% of each run, Pallas kernels for 0% -> 5%
where the time goes in v1:
time: 613 us; the launch traced here: 604 us
  starting transfers between devices  193 us (31%)
  local copies, waits for them, and re-layouts  129 us (21%)
  waiting for transfers between devices  126 us (21%)
  Pallas kernels  61.8 us (10%)
  other arithmetic  50.7 us (8%)
  matrix products  40.1 us (7%)
    ppermute x109, starting transfers between devices, fetch(): return lax.ppermute(array, ('seq', 'batch'), shift_pairs(axis, step))  193 us
    ppermute x109, waiting for transfers between devices, fetch(): return lax.ppermute(array, ('seq', 'batch'), shift_pairs(axis, step))  126 us
    unnamed x169, local copies, waits for them, and re-layouts  58 us
    pallas_call x1, Pallas kernels, attend_back(): pl.pallas_call(bwd_kernel, grid_spec=pltpu.PrefetchScalarGridSpec(num_sca...  31.9 us
    pallas_call x1, Pallas kernels, attend(): pl.pallas_call(fwd_kernel, grid_spec=pltpu.PrefetchScalarGridSpec(num_sca...  29.9 us
    dot_general x5, matrix products, tn(): lax.dot_general(left, right, (((0,), (0,)), ((), ())), preferred_element_...  14 us
    another operation x4, other arithmetic, roll_slots(): stacked = jnp.stack(pieces + pieces[:-1])  12.7 us
    dynamic_slice x4, local copies, waits for them, and re-layouts, halves(): own = lax.dynamic_index_in_dim(parts, c, 1, keepdims=False)  12.7 us
  transfers between devices with their start and end apart: 109, of which 46 were waited for; matrix products, arithmetic and copies ran while one was open for 30% of the time, Pallas kernels for 5%

profile of v1, /device:TPU:10, one launch (start us, length us, event | category | flops | bytes accessed | tf_op | source)
XLA Modules:
  0.0 604.1 jit_solution(5489422964271059862)
XLA Ops:
  4.9 3.9 collective-permute-start
  10.4 3.5 collective-permute-start.3
  15.9 3.5 collective-permute-start.2
  19.4 11.8 %collective-permute-start.4 = (bf16[256,768]{1,0:T(8,128)(2,1)S(1)}, bf16[256,768]{1,0:T(8,128)(2,1)S(1)}, u32[]{:S(2)}, u32[]{:S(2)}) collective-permute-start(bf16[256,768]{1,0:T(8,128)(2,1)S(1)} %collective-permute-done), channel_id=1, source_target_pairs={{64,0},{65,1},{66,2},{67,3},{68,4},{69,5},{70,6},{71,7},{72,8},{73... | collective-permute-start | bytes 1179656 | tf_op jit(solution)/shard_map/ppermute | solution.py:34
  34.3 4.9 collective-permute-done.4
  43.7 5.8 copy.52
  53.0 3.4 pad_maximum_fusion
  59.7 4.0 add_convert_fusion
  63.7 4.6 copy.58.kv_ref
  70.2 29.9 %attend.1 = (bf16[4,256,192]{2,1,0:T(8,128)(2,1)S(1)}, f32[4,256,192]{2,1,0:T(8,128)S(1)}, f32[4,3,256]{2,1,0:T(4,128)S(1)}) custom-call(s32[16]{0:T(128)S(1)} %scatter_custom_fusion.slot_of, s32[4]{0:T(128)S(1)} %slice.104.block_of, bf16[4,256,192]{2,1,0:T(8,128)(2,1)S(1)} %fusion.35.q_ref, bf16[16,256,384]{2,1,0:T(8,128)(2,1)S(1)} %copy-done.2, ...), custom_call_target="tpu_custom_call" | custom-call | tf_op jit(solution)/shard_map/attend/pallas_call | solution.py:161
  102.4 7.4 %collective-permute-start.8 = (bf16[256,192]{1,0:T(8,128)(2,1)}, bf16[256,192]{1,0:T(8,128)(2,1)S(1)}, u32[]{:S(2)}, u32[]{:S(2)}) collective-permute-start(bf16[256,192]{1,0:T(8,128)(2,1)} %get-tuple-element.103), channel_id=1, source_target_pairs={{32,0},{33,1},{34,2},{35,3},{36,4},{37,5},{38,6},{39,7},{40,8},{41... | collective-permute-start | bytes 294920 | tf_op jit(solution)/shard_map/ppermute | solution.py:34
  109.7 4.0 collective-permute-start.89
  115.7 5.0 collective-permute-done.9
  122.8 6.0 multiply_convert_fusion
  128.8 4.2 convert_reduce_fusion
  139.5 5.0 reshape.413
  146.3 3.9 collective-permute-start.12
  150.9 5.0 reshape.421
  155.9 7.0 %constant_dynamic-slice_fusion.6 = (bf16[256,1,1536]{2,1,0:T(2,128)(2,1)}, bf16[256,1,1536]{2,1,0:T(2,128)(2,1)}) fusion(bf16[256,2,1536]{2,1,0:T(2,128)(2,1)} %reshape.421, s32[]{:T(128)S(6)} %select_n.156, s32[]{:T(128)S(6)} %select_n.170), kind=kLoop, calls=%fused_computation.341 | loop fusion | bytes 3145736 | tf_op jit(solution)/shard_map/jit(dynamic_index_in_dim)/dynamic_slice | solution.py:307
  162.9 4.9 constant_dynamic-slice_fusion.11
  172.5 31.9 %attend_back.1 = (bf16[4,256,192]{2,1,0:T(8,128)(2,1)}, f32[16,256,384]{2,1,0:T(8,128)}) custom-call(s32[16]{0:T(128)} %copy-done.7, s32[4]{0:T(128)} %copy-done.6, bf16[4,256,192]{2,1,0:T(8,128)(2,1)} %copy-done.3, bf16[4,256,192]{2,1,0:T(8,128)(2,1)} %pad_maximum_fusion.3.do_ref, f32[4,256,192]{2,1,0:T(8,128)} %copy-done.4, f32[4,3,256]{2,1,0:T(4,128)} %copy-done.5, ...), custom_call_target="tpu_custom_call" | custom-call | tf_op jit(solution)/shard_map/attend_back/pallas_call | solution.py:185
  204.4 4.9 convert_element_type.358
  209.3 4.8 copy.71
  214.1 6.4 %convolution_convert_fusion.2 = bf16[3,2,64,768]{3,2,1,0:T(8,128)(2,1)S(1)} fusion(bf16[3,2,64,4096]{3,2,1,0:T(8,128)(2,1)} %bitcast.531, bf16[4096,768,1,1]{1,0,3,2:T(8,128)(2,1)} %bitcast.509), kind=kOutput, calls=%fused_computation.54 | convolution fusion | flops 2416214016 | bytes 10027008 | tf_op jit(solution)/shard_map/dot_general | solution.py:314
  222.7 3.4 collective-permute-start.29
  226.1 4.5 fusion.41
  242.9 16.8 %collective-permute-start.35 = (bf16[24,768]{1,0:T(8,128)(2,1)}, bf16[24,768]{1,0:T(8,128)(2,1)S(1)}, u32[]{:S(2)}, u32[]{:S(2)}) collective-permute-start(bf16[24,768]{1,0:T(8,128)(2,1)} %get-tuple-element.124), channel_id=1, source_target_pairs={{4,0},{5,1},{6,2},{7,3},{16,4},{17,5},{18,6},{19,7},{12,8},{13,9},... | collective-permute-start | bytes 110600 | tf_op jit(solution)/shard_map/ppermute | solution.py:34
  261.0 4.0 fusion.156
  280.1 3.5 collective-permute-done.37
  285.5 3.2 collective-permute-done.38
  290.4 3.0 collective-permute-start.41
  305.7 6.8 %collective-permute-done.92 = bf16[384,768]{1,0:T(8,128)(2,1)S(1)} collective-permute-done((bf16[384,768]{1,0:T(8,128)(2,1)S(1)}, bf16[384,768]{1,0:T(8,128)(2,1)S(1)}, u32[]{:S(2)}, u32[]{:S(2)}) %collective-permute-start.92) | collective-permute-done | bytes 589856 | tf_op jit(solution)/shard_map/ppermute | solution.py:34
  314.7 6.4 %collective-permute-done.91 = bf16[384,768]{1,0:T(8,128)(2,1)S(1)} collective-permute-done((bf16[384,768]{1,0:T(8,128)(2,1)S(1)}, bf16[384,768]{1,0:T(8,128)(2,1)S(1)}, u32[]{:S(2)}, u32[]{:S(2)}) %collective-permute-start.91) | collective-permute-done | bytes 589856 | tf_op jit(solution)/shard_map/ppermute | solution.py:34
  322.2 4.9 collective-permute-done.90
  338.8 3.1 collective-permute-start.43
  342.0 2.9 collective-permute-start.74
  354.6 2.9 collective-permute-done.52
  379.3 3.8 collective-permute-done.58
  383.5 4.4 collective-permute-done.59
  391.9 3.2 collective-permute-start.79
  397.4 10.5 %collective-permute-start.80 = (bf16[24,768]{1,0:T(8,128)(2,1)S(1)}, bf16[24,768]{1,0:T(8,128)(2,1)S(1)}, u32[]{:S(2)}, u32[]{:S(2)}) collective-permute-start(bf16[24,768]{1,0:T(8,128)(2,1)S(1)} %get-tuple-element.58), channel_id=1, source_target_pairs={{96,0},{97,1},{98,2},{99,3},{100,4},{101,5},{102,6},{103,7},{104,8... | collective-permute-start | bytes 110600 | tf_op jit(solution)/shard_map/ppermute | solution.py:34
  410.4 3.2 collective-permute-start.99
  417.0 3.7 collective-permute-done.100
  421.8 4.4 collective-permute-done.101
  426.2 3.2 collective-permute-start.60
  431.0 3.3 collective-permute-start.61
  437.5 3.6 collective-permute-done.62
  441.1 3.2 collective-permute-start.81
  451.2 2.8 collective-permute-start.102
  457.8 2.9 collective-permute-done.103
  479.1 2.7 collective-permute-start.105
  486.6 3.4 copy.73
  490.0 8.0 %copy.82 = f32[768,2304]{1,0:T(8,128)} copy(f32[768,2304]{0,1:T(8,128)} %bitcast.495) | data formatting | bytes 14155776
  512.1 3.2 constant_dynamic-slice_fusion.7
  522.9 12.2 %collective-permute-done.16 = bf16[256,576]{0,1:T(8,128)(2,1)S(1)} collective-permute-done((bf16[256,576]{0,1:T(8,128)(2,1)S(1)}, bf16[256,576]{0,1:T(8,128)(2,1)S(1)}, u32[]{:S(2)}, u32[]{:S(2)}) %collective-permute-start.16) | collective-permute-done | bytes 294944 | tf_op jit(solution)/shard_map/ppermute | solution.py:34
  535.1 8.1 %collective-permute-done.18 = bf16[256,576]{0,1:T(8,128)(2,1)S(1)} collective-permute-done((bf16[256,576]{0,1:T(8,128)(2,1)S(1)}, bf16[256,576]{0,1:T(8,128)(2,1)S(1)}, u32[]{:S(2)}, u32[]{:S(2)}) %collective-permute-start.18) | collective-permute-done | bytes 294944 | tf_op jit(solution)/shard_map/ppermute | solution.py:34
  554.0 3.7 collective-permute-done.20
  561.8 2.9 collective-permute-done.25
  570.1 3.0 collective-permute-done.26
  574.4 5.1 fusion.3
  579.5 4.8 bitcast_convert_fusion.1
  584.3 9.6 %copy.79 = f32[3072,768]{0,1:T(8,128)} copy(f32[3072,768]{1,0:T(8,128)} %bitcast_convert_fusion.1) | data formatting | bytes 18874368 | tf_op jit(solution)/shard_map/convert_element_type | solution.py:334
  593.8 5.0 fusion.1
  598.8 4.8 bitcast_convert_fusion
  (501 shorter events, 231.6 us)
Async XLA Ops:
  4.4 11.5 %collective-permute-start.1 = (bf16[256,768]{1,0:T(8,128)(2,1)S(1)}, bf16[256,768]{1,0:T(8,128)(2,1)S(1)}, u32[]{:S(2)}, u32[]{:S(2)}) collective-permute-start(bf16[256,768]{1,0:T(8,128)(2,1)S(1)} %fusion.67), channel_id=1, source_target_pairs={{32,0},{33,1},{34,2},{35,3},{36,4},{37,5},{38,6},{39,7},{40,8},{41... | collective-permute-start | bytes 1179656 | tf_op jit(solution)/shard_map/ppermute | solution.py:34
  4.9 14.4 %collective-permute-start = (bf16[256,768]{1,0:T(8,128)(2,1)S(1)}, bf16[256,768]{1,0:T(8,128)(2,1)S(1)}, u32[]{:S(2)}, u32[]{:S(2)}) collective-permute-start(bf16[256,768]{1,0:T(8,128)(2,1)S(1)} %fusion.67), channel_id=1, source_target_pairs={{16,0},{17,1},{18,2},{19,3},{20,4},{21,5},{22,6},{23,7},{24,8},{25... | collective-permute-start | bytes 1179656 | tf_op jit(solution)/shard_map/ppermute | solution.py:34
  8.8 22.3 %collective-permute-start.5 = (bf16[256,768]{1,0:T(8,128)(2,1)S(1)}, bf16[256,768]{1,0:T(8,128)(2,1)S(1)}, u32[]{:S(2)}, u32[]{:S(2)}) collective-permute-start(bf16[256,768]{1,0:T(8,128)(2,1)S(1)} %fusion.67), channel_id=1, source_target_pairs={{96,0},{97,1},{98,2},{99,3},{100,4},{101,5},{102,6},{103,7},{104,8... | collective-permute-start | bytes 1179656 | tf_op jit(solution)/shard_map/ppermute | solution.py:34
  10.4 23.1 %collective-permute-start.3 = (bf16[256,768]{1,0:T(8,128)(2,1)S(1)}, bf16[256,768]{1,0:T(8,128)(2,1)S(1)}, u32[]{:S(2)}, u32[]{:S(2)}) collective-permute-start(bf16[256,768]{1,0:T(8,128)(2,1)S(1)} %fusion.67), channel_id=1, source_target_pairs={{64,0},{65,1},{66,2},{67,3},{68,4},{69,5},{70,6},{71,7},{72,8},{73... | collective-permute-start | bytes 1179656 | tf_op jit(solution)/shard_map/ppermute | solution.py:34
  15.9 16.8 %collective-permute-start.2 = (bf16[256,768]{1,0:T(8,128)(2,1)S(1)}, bf16[256,768]{1,0:T(8,128)(2,1)S(1)}, u32[]{:S(2)}, u32[]{:S(2)}) collective-permute-start(bf16[256,768]{1,0:T(8,128)(2,1)S(1)} %collective-permute-done.1), channel_id=1, source_target_pairs={{16,0},{17,1},{18,2},{19,3},{20,4},{21,5},{22,6},{23,7},{24,8},{25... | collective-permute-start | bytes 1179656 | tf_op jit(solution)/shard_map/ppermute | solution.py:34
  19.4 19.8 %collective-permute-start.4 = (bf16[256,768]{1,0:T(8,128)(2,1)S(1)}, bf16[256,768]{1,0:T(8,128)(2,1)S(1)}, u32[]{:S(2)}, u32[]{:S(2)}) collective-permute-start(bf16[256,768]{1,0:T(8,128)(2,1)S(1)} %collective-permute-done), channel_id=1, source_target_pairs={{64,0},{65,1},{66,2},{67,3},{68,4},{69,5},{70,6},{71,7},{72,8},{73... | collective-permute-start | bytes 1179656 | tf_op jit(solution)/shard_map/ppermute | solution.py:34
  31.2 10.9 %collective-permute-start.6 = (bf16[256,768]{1,0:T(8,128)(2,1)S(1)}, bf16[256,768]{1,0:T(8,128)(2,1)S(1)}, u32[]{:S(2)}, u32[]{:S(2)}) collective-permute-start(bf16[256,768]{1,0:T(8,128)(2,1)S(1)} %collective-permute-done.5), channel_id=1, source_target_pairs={{16,0},{17,1},{18,2},{19,3},{20,4},{21,5},{22,6},{23,7},{24,8},{25... | collective-permute-start | bytes 1179656 | tf_op jit(solution)/shard_map/ppermute | solution.py:34
  42.9 10.1 %collective-permute-start.7 = (bf16[8,256,768]{2,1,0:T(8,128)(2,1)}, bf16[8,256,768]{2,1,0:T(8,128)(2,1)}, u32[]{:S(2)}, u32[]{:S(2)}) collective-permute-start(bf16[8,256,768]{2,1,0:T(8,128)(2,1)} %bitcast_dynamic-update-slice_fusion.21), channel_id=1, source_target_pairs={{8,0},{9,1},{10,2},{11,3},{12,4},{13,5},{14,6},{15,7},{0,8},{1,9},... | collective-permute-start | bytes 9437192 | tf_op jit(solution)/shard_map/ppermute | solution.py:34
  102.4 13.3 %collective-permute-start.8 = (bf16[256,192]{1,0:T(8,128)(2,1)}, bf16[256,192]{1,0:T(8,128)(2,1)S(1)}, u32[]{:S(2)}, u32[]{:S(2)}) collective-permute-start(bf16[256,192]{1,0:T(8,128)(2,1)} %get-tuple-element.103), channel_id=1, source_target_pairs={{32,0},{33,1},{34,2},{35,3},{36,4},{37,5},{38,6},{39,7},{40,8},{41... | collective-permute-start | bytes 294920 | tf_op jit(solution)/shard_map/ppermute | solution.py:34
  109.7 179.7 %collective-permute-start.89 = (bf16[256,768]{1,0:T(8,128)(2,1)}, bf16[256,768]{1,0:T(8,128)(2,1)}, u32[]{:S(2)}, u32[]{:S(2)}) collective-permute-start(bf16[256,768]{1,0:T(8,128)(2,1)} %bitcast.31), channel_id=1, source_target_pairs={{8,0},{9,1},{10,2},{11,3},{12,4},{13,5},{14,6},{15,7},{0,8},{1,9},... | collective-permute-start | bytes 1179656 | tf_op jit(solution)/shard_map/ppermute | solution.py:34
  113.7 6.9 %collective-permute-start.9 = (bf16[256,192]{1,0:T(8,128)(2,1)S(1)}, bf16[256,192]{1,0:T(8,128)(2,1)S(1)}, u32[]{:S(2)}, u32[]{:S(2)}) collective-permute-start(bf16[256,192]{1,0:T(8,128)(2,1)S(1)} %get-tuple-element.102), channel_id=1, source_target_pairs={{64,0},{65,1},{66,2},{67,3},{68,4},{69,5},{70,6},{71,7},{72,8},{73... | collective-permute-start | bytes 294920 | tf_op jit(solution)/shard_map/ppermute | solution.py:34
  113.7 6.9 %collective-permute-start.10 = (bf16[256,192]{1,0:T(8,128)(2,1)S(1)}, bf16[256,192]{1,0:T(8,128)(2,1)S(1)}, u32[]{:S(2)}, u32[]{:S(2)}) collective-permute-start(bf16[256,192]{1,0:T(8,128)(2,1)S(1)} %get-tuple-element.100), channel_id=1, source_target_pairs={{96,0},{97,1},{98,2},{99,3},{100,4},{101,5},{102,6},{103,7},{104,8... | collective-permute-start | bytes 294920 | tf_op jit(solution)/shard_map/ppermute | solution.py:34
  139.5 134.4 %collective-permute-start.47 = (bf16[256,768]{1,0:T(8,128)(2,1)}, bf16[256,768]{1,0:T(8,128)(2,1)}, u32[]{:S(2)}, u32[]{:S(2)}) collective-permute-start(bf16[256,768]{1,0:T(8,128)(2,1)} %get-tuple-element.64), channel_id=1, source_target_pairs={{8,0},{9,1},{10,2},{11,3},{12,4},{13,5},{14,6},{15,7},{0,8},{1,9},... | collective-permute-start | bytes 1179656 | tf_op jit(solution)/shard_map/ppermute | solution.py:34
  144.9 26.6 %collective-permute-start.13 = (bf16[256,192]{1,0:T(8,128)(2,1)S(1)}, bf16[256,192]{1,0:T(8,128)(2,1)S(1)}, u32[]{:S(2)}, u32[]{:S(2)}) collective-permute-start(bf16[256,192]{1,0:T(8,128)(2,1)S(1)} %bitcast.590), channel_id=1, source_target_pairs={{96,0},{97,1},{98,2},{99,3},{100,4},{101,5},{102,6},{103,7},{104,8... | collective-permute-start | bytes 294920 | tf_op jit(solution)/shard_map/ppermute | solution.py:34
  146.3 25.2 %collective-permute-start.12 = (bf16[256,192]{1,0:T(8,128)(2,1)S(1)}, bf16[256,192]{1,0:T(8,128)(2,1)S(1)}, u32[]{:S(2)}, u32[]{:S(2)}) collective-permute-start(bf16[256,192]{1,0:T(8,128)(2,1)S(1)} %bitcast.591), channel_id=1, source_target_pairs={{64,0},{65,1},{66,2},{67,3},{68,4},{69,5},{70,6},{71,7},{72,8},{73... | collective-permute-start | bytes 294920 | tf_op jit(solution)/shard_map/ppermute | solution.py:34
  150.4 21.1 %collective-permute-start.11 = (bf16[256,192]{1,0:T(8,128)(2,1)S(1)}, bf16[256,192]{1,0:T(8,128)(2,1)S(1)}, u32[]{:S(2)}, u32[]{:S(2)}) collective-permute-start(bf16[256,192]{1,0:T(8,128)(2,1)S(1)} %bitcast.592), channel_id=1, source_target_pairs={{32,0},{33,1},{34,2},{35,3},{36,4},{37,5},{38,6},{39,7},{40,8},{41... | collective-permute-start | bytes 294920 | tf_op jit(solution)/shard_map/ppermute | solution.py:34
  222.7 7.9 %collective-permute-start.29 = (bf16[288,768]{1,0:T(8,128)(2,1)S(1)}, bf16[288,768]{1,0:T(8,128)(2,1)S(1)}, u32[]{:S(2)}, u32[]{:S(2)}) collective-permute-start(bf16[288,768]{1,0:T(8,128)(2,1)S(1)} %dynamic-slice_bitcast_fusion.7), channel_id=1, source_target_pairs={{8,0},{9,1},{10,2},{11,3},{12,4},{13,5},{14,6},{15,7},{0,8},{1,9},... | collective-permute-start | bytes 1327112 | tf_op jit(solution)/shard_map/ppermute | solution.py:34
  230.8 11.3 %collective-permute-start.32 = (bf16[72,768]{1,0:T(8,128)(2,1)S(1)}, bf16[72,768]{1,0:T(8,128)(2,1)S(1)}, u32[]{:S(2)}, u32[]{:S(2)}) collective-permute-start(bf16[72,768]{1,0:T(8,128)(2,1)S(1)} %get-tuple-element.105), channel_id=1, source_target_pairs={{1,0},{2,1},{3,2},{0,3},{5,4},{6,5},{7,6},{4,7},{9,8},{10,9},{11,1... | collective-permute-start | bytes 331784 | tf_op jit(solution)/shard_map/ppermute | solution.py:34
  231.4 10.7 %collective-permute-start.31 = (bf16[72,768]{1,0:T(8,128)(2,1)S(1)}, bf16[72,768]{1,0:T(8,128)(2,1)S(1)}, u32[]{:S(2)}, u32[]{:S(2)}) collective-permute-start(bf16[72,768]{1,0:T(8,128)(2,1)S(1)} %get-tuple-element.106), channel_id=1, source_target_pairs={{2,0},{3,1},{0,2},{1,3},{6,4},{7,5},{4,6},{5,7},{10,8},{11,9},{8,1... | collective-permute-start | bytes 331784 | tf_op jit(solution)/shard_map/ppermute | solution.py:34
  233.8 8.3 %collective-permute-start.30 = (bf16[72,768]{1,0:T(8,128)(2,1)S(1)}, bf16[72,768]{1,0:T(8,128)(2,1)S(1)}, u32[]{:S(2)}, u32[]{:S(2)}) collective-permute-start(bf16[72,768]{1,0:T(8,128)(2,1)S(1)} %get-tuple-element.104), channel_id=1, source_target_pairs={{3,0},{0,1},{1,2},{2,3},{7,4},{4,5},{5,6},{6,7},{11,8},{8,9},{9,10... | collective-permute-start | bytes 331784 | tf_op jit(solution)/shard_map/ppermute | solution.py:34
  242.9 27.7 %collective-permute-start.35 = (bf16[24,768]{1,0:T(8,128)(2,1)}, bf16[24,768]{1,0:T(8,128)(2,1)S(1)}, u32[]{:S(2)}, u32[]{:S(2)}) collective-permute-start(bf16[24,768]{1,0:T(8,128)(2,1)} %get-tuple-element.124), channel_id=1, source_target_pairs={{4,0},{5,1},{6,2},{7,3},{16,4},{17,5},{18,6},{19,7},{12,8},{13,9},... | collective-permute-start | bytes 110600 | tf_op jit(solution)/shard_map/ppermute | solution.py:34
  259.7 10.9 %collective-permute-start.34 = (bf16[24,768]{1,0:T(8,128)(2,1)S(1)}, bf16[24,768]{1,0:T(8,128)(2,1)S(1)}, u32[]{:S(2)}, u32[]{:S(2)}) collective-permute-start(bf16[24,768]{1,0:T(8,128)(2,1)S(1)} %get-tuple-element.125), channel_id=1, source_target_pairs={{16,0},{17,1},{18,2},{19,3},{20,4},{21,5},{22,6},{23,7},{24,8},{25... | collective-permute-start | bytes 110600 | tf_op jit(solution)/shard_map/ppermute | solution.py:34
  259.7 11.4 %collective-permute-start.33 = (bf16[24,768]{1,0:T(8,128)(2,1)S(1)}, bf16[24,768]{1,0:T(8,128)(2,1)S(1)}, u32[]{:S(2)}, u32[]{:S(2)}) collective-permute-start(bf16[24,768]{1,0:T(8,128)(2,1)S(1)} %get-tuple-element.123), channel_id=1, source_target_pairs={{20,0},{21,1},{22,2},{23,3},{0,4},{1,5},{2,6},{3,7},{28,8},{29,9},... | collective-permute-start | bytes 110600 | tf_op jit(solution)/shard_map/ppermute | solution.py:34
  270.6 28.1 %collective-permute-start.68 = (bf16[256,768]{1,0:T(8,128)(2,1)S(1)}, bf16[256,768]{1,0:T(8,128)(2,1)S(1)}, u32[]{:S(2)}, u32[]{:S(2)}) collective-permute-start(bf16[256,768]{1,0:T(8,128)(2,1)S(1)} %copy-done.25), channel_id=1, source_target_pairs={{8,0},{9,1},{10,2},{11,3},{12,4},{13,5},{14,6},{15,7},{0,8},{1,9},... | collective-permute-start | bytes 1179656 | tf_op jit(solution)/shard_map/ppermute | solution.py:34
  270.6 19.8 %collective-permute-start.88 = (bf16[256,1536]{1,0:T(8,128)(2,1)S(1)}, bf16[256,1536]{1,0:T(8,128)(2,1)S(1)}, u32[]{:S(2)}, u32[]{:S(2)}) collective-permute-start(bf16[256,1536]{1,0:T(8,128)(2,1)S(1)} %bitcast.571), channel_id=1, source_target_pairs={{8,0},{9,1},{10,2},{11,3},{12,4},{13,5},{14,6},{15,7},{0,8},{1,9},... | collective-permute-start | bytes 2359304 | tf_op jit(solution)/shard_map/ppermute | solution.py:34
  273.7 27.5 %collective-permute-start.67 = (bf16[256,1536]{1,0:T(8,128)(2,1)}, bf16[256,1536]{1,0:T(8,128)(2,1)S(1)}, u32[]{:S(2)}, u32[]{:S(2)}) collective-permute-start(bf16[256,1536]{1,0:T(8,128)(2,1)} %bitcast.573), channel_id=1, source_target_pairs={{8,0},{9,1},{10,2},{11,3},{12,4},{13,5},{14,6},{15,7},{0,8},{1,9},... | collective-permute-start | bytes 2359304 | tf_op jit(solution)/shard_map/ppermute | solution.py:34
  288.7 7.3 %collective-permute-start.39 = (bf16[72,768]{1,0:T(8,128)(2,1)S(1)}, bf16[72,768]{1,0:T(8,128)(2,1)S(1)}, u32[]{:S(2)}, u32[]{:S(2)}) collective-permute-start(bf16[72,768]{1,0:T(8,128)(2,1)S(1)} %bitcast.565), channel_id=1, source_target_pairs={{1,0},{2,1},{3,2},{0,3},{5,4},{6,5},{7,6},{4,7},{9,8},{10,9},{11,1... | collective-permute-start | bytes 331784 | tf_op jit(solution)/shard_map/ppermute | solution.py:34
  289.4 6.8 %collective-permute-start.40 = (bf16[72,768]{1,0:T(8,128)(2,1)S(1)}, bf16[72,768]{1,0:T(8,128)(2,1)S(1)}, u32[]{:S(2)}, u32[]{:S(2)}) collective-permute-start(bf16[72,768]{1,0:T(8,128)(2,1)S(1)} %bitcast.567), channel_id=1, source_target_pairs={{2,0},{3,1},{0,2},{1,3},{6,4},{7,5},{4,6},{5,7},{10,8},{11,9},{8,1... | collective-permute-start | bytes 331784 | tf_op jit(solution)/shard_map/ppermute | solution.py:34
  296.0 16.4 %collective-permute-start.92 = (bf16[384,768]{1,0:T(8,128)(2,1)S(1)}, bf16[384,768]{1,0:T(8,128)(2,1)S(1)}, u32[]{:S(2)}, u32[]{:S(2)}) collective-permute-start(bf16[384,768]{1,0:T(8,128)(2,1)S(1)} %get-tuple-element.74), channel_id=1, source_target_pairs={{1,0},{2,1},{3,2},{0,3},{5,4},{6,5},{7,6},{4,7},{9,8},{10,9},{11,1... | collective-permute-start | bytes 1769480 | tf_op jit(solution)/shard_map/ppermute | solution.py:34
  297.0 7.6 %collective-permute-start.42 = (bf16[288,768]{1,0:T(8,128)(2,1)S(1)}, bf16[288,768]{1,0:T(8,128)(2,1)S(1)}, u32[]{:S(2)}, u32[]{:S(2)}) collective-permute-start(bf16[288,768]{1,0:T(8,128)(2,1)S(1)} %bitcast.543), channel_id=1, source_target_pairs={{8,0},{9,1},{10,2},{11,3},{12,4},{13,5},{14,6},{15,7},{0,8},{1,9},... | collective-permute-start | bytes 1327112 | tf_op jit(solution)/shard_map/ppermute | solution.py:34
  297.2 23.9 %collective-permute-start.91 = (bf16[384,768]{1,0:T(8,128)(2,1)S(1)}, bf16[384,768]{1,0:T(8,128)(2,1)S(1)}, u32[]{:S(2)}, u32[]{:S(2)}) collective-permute-start(bf16[384,768]{1,0:T(8,128)(2,1)S(1)} %get-tuple-element.75), channel_id=1, source_target_pairs={{2,0},{3,1},{0,2},{1,3},{6,4},{7,5},{4,6},{5,7},{10,8},{11,9},{8,1... | collective-permute-start | bytes 1769480 | tf_op jit(solution)/shard_map/ppermute | solution.py:34
  298.7 28.5 %collective-permute-start.90 = (bf16[384,768]{1,0:T(8,128)(2,1)S(1)}, bf16[384,768]{1,0:T(8,128)(2,1)S(1)}, u32[]{:S(2)}, u32[]{:S(2)}) collective-permute-start(bf16[384,768]{1,0:T(8,128)(2,1)S(1)} %get-tuple-element.73), channel_id=1, source_target_pairs={{3,0},{0,1},{1,2},{2,3},{7,4},{4,5},{5,6},{6,7},{11,8},{8,9},{9,10... | collective-permute-start | bytes 1769480 | tf_op jit(solution)/shard_map/ppermute | solution.py:34
  302.8 27.4 %collective-permute-start.71 = (bf16[384,768]{1,0:T(8,128)(2,1)S(1)}, bf16[384,768]{1,0:T(8,128)(2,1)S(1)}, u32[]{:S(2)}, u32[]{:S(2)}) collective-permute-start(bf16[384,768]{1,0:T(8,128)(2,1)S(1)} %get-tuple-element.77), channel_id=1, source_target_pairs={{4,0},{5,1},{6,2},{7,3},{16,4},{17,5},{18,6},{19,7},{12,8},{13,9},... | collective-permute-start | bytes 1769480 | tf_op jit(solution)/shard_map/ppermute | solution.py:34
  304.6 26.8 %collective-permute-start.70 = (bf16[384,768]{1,0:T(8,128)(2,1)S(1)}, bf16[384,768]{1,0:T(8,128)(2,1)S(1)}, u32[]{:S(2)}, u32[]{:S(2)}) collective-permute-start(bf16[384,768]{1,0:T(8,128)(2,1)S(1)} %get-tuple-element.78), channel_id=1, source_target_pairs={{16,0},{17,1},{18,2},{19,3},{20,4},{21,5},{22,6},{23,7},{24,8},{25... | collective-permute-start | bytes 1769480 | tf_op jit(solution)/shard_map/ppermute | solution.py:34
  312.5 21.2 %collective-permute-start.69 = (bf16[384,768]{1,0:T(8,128)(2,1)S(1)}, bf16[384,768]{1,0:T(8,128)(2,1)S(1)}, u32[]{:S(2)}, u32[]{:S(2)}) collective-permute-start(bf16[384,768]{1,0:T(8,128)(2,1)S(1)} %get-tuple-element.76), channel_id=1, source_target_pairs={{20,0},{21,1},{22,2},{23,3},{0,4},{1,5},{2,6},{3,7},{28,8},{29,9},... | collective-permute-start | bytes 1769480 | tf_op jit(solution)/shard_map/ppermute | solution.py:34
  321.0 7.4 %collective-permute-start.50 = (bf16[96,768]{1,0:T(8,128)(2,1)S(1)}, bf16[96,768]{1,0:T(8,128)(2,1)S(1)}, u32[]{:S(2)}, u32[]{:S(2)}) collective-permute-start(bf16[96,768]{1,0:T(8,128)(2,1)S(1)} %get-tuple-element.96), channel_id=1, source_target_pairs={{32,0},{33,1},{34,2},{35,3},{36,4},{37,5},{38,6},{39,7},{40,8},{41... | collective-permute-start | bytes 442376 | tf_op jit(solution)/shard_map/ppermute | solution.py:34
  327.1 9.3 %collective-permute-start.49 = (bf16[96,768]{1,0:T(8,128)(2,1)S(1)}, bf16[96,768]{1,0:T(8,128)(2,1)S(1)}, u32[]{:S(2)}, u32[]{:S(2)}) collective-permute-start(bf16[96,768]{1,0:T(8,128)(2,1)S(1)} %get-tuple-element.97), channel_id=1, source_target_pairs={{64,0},{65,1},{66,2},{67,3},{68,4},{69,5},{70,6},{71,7},{72,8},{73... | collective-permute-start | bytes 442376 | tf_op jit(solution)/shard_map/ppermute | solution.py:34
  328.4 10.4 %collective-permute-start.48 = (bf16[96,768]{1,0:T(8,128)(2,1)S(1)}, bf16[96,768]{1,0:T(8,128)(2,1)S(1)}, u32[]{:S(2)}, u32[]{:S(2)}) collective-permute-start(bf16[96,768]{1,0:T(8,128)(2,1)S(1)} %get-tuple-element.95), channel_id=1, source_target_pairs={{96,0},{97,1},{98,2},{99,3},{100,4},{101,5},{102,6},{103,7},{104,8... | collective-permute-start | bytes 442376 | tf_op jit(solution)/shard_map/ppermute | solution.py:34
  330.2 11.8 %collective-permute-start.95 = (bf16[96,768]{1,0:T(8,128)(2,1)S(1)}, bf16[96,768]{1,0:T(8,128)(2,1)S(1)}, u32[]{:S(2)}, u32[]{:S(2)}) collective-permute-start(bf16[96,768]{1,0:T(8,128)(2,1)S(1)} %get-tuple-element.90), channel_id=1, source_target_pairs={{32,0},{33,1},{34,2},{35,3},{36,4},{37,5},{38,6},{39,7},{40,8},{41... | collective-permute-start | bytes 442376 | tf_op jit(solution)/shard_map/ppermute | solution.py:34
  331.5 13.4 %collective-permute-start.94 = (bf16[96,768]{1,0:T(8,128)(2,1)S(1)}, bf16[96,768]{1,0:T(8,128)(2,1)S(1)}, u32[]{:S(2)}, u32[]{:S(2)}) collective-permute-start(bf16[96,768]{1,0:T(8,128)(2,1)S(1)} %get-tuple-element.91), channel_id=1, source_target_pairs={{64,0},{65,1},{66,2},{67,3},{68,4},{69,5},{70,6},{71,7},{72,8},{73... | collective-permute-start | bytes 442376 | tf_op jit(solution)/shard_map/ppermute | solution.py:34
  333.6 11.7 %collective-permute-start.93 = (bf16[96,768]{1,0:T(8,128)(2,1)S(1)}, bf16[96,768]{1,0:T(8,128)(2,1)S(1)}, u32[]{:S(2)}, u32[]{:S(2)}) collective-permute-start(bf16[96,768]{1,0:T(8,128)(2,1)S(1)} %get-tuple-element.89), channel_id=1, source_target_pairs={{96,0},{97,1},{98,2},{99,3},{100,4},{101,5},{102,6},{103,7},{104,8... | collective-permute-start | bytes 442376 | tf_op jit(solution)/shard_map/ppermute | solution.py:34
  336.4 108.0 %collective-permute-start.14 = (bf16[4,2,256,384]{2,3,0,1:T(8,128)(2,1)}, bf16[4,2,256,384]{2,3,0,1:T(8,128)(2,1)}, u32[]{:S(2)}, u32[]{:S(2)}) collective-permute-start(bf16[4,2,256,384]{2,3,0,1:T(8,128)(2,1)} %bitcast.42), channel_id=1, source_target_pairs={{8,0},{9,1},{10,2},{11,3},{12,4},{13,5},{14,6},{15,7},{0,8},{1,9},... | collective-permute-start | bytes 4718600 | tf_op jit(solution)/shard_map/ppermute | solution.py:34
  338.8 135.2 %collective-permute-start.43 = (bf16[576,768]{1,0:T(8,128)(2,1)S(1)}, bf16[576,768]{1,0:T(8,128)(2,1)}, u32[]{:S(2)}, u32[]{:S(2)}) collective-permute-start(bf16[576,768]{1,0:T(8,128)(2,1)S(1)} %bitcast.503), channel_id=1, source_target_pairs={{32,0},{33,1},{34,2},{35,3},{36,4},{37,5},{38,6},{39,7},{40,8},{41... | collective-permute-start | bytes 2654216 | tf_op jit(solution)/shard_map/ppermute | solution.py:34
  344.9 7.1 %collective-permute-start.73 = (bf16[96,768]{1,0:T(8,128)(2,1)S(1)}, bf16[96,768]{1,0:T(8,128)(2,1)S(1)}, u32[]{:S(2)}, u32[]{:S(2)}) collective-permute-start(bf16[96,768]{1,0:T(8,128)(2,1)S(1)} %get-tuple-element.94), channel_id=1, source_target_pairs={{2,0},{3,1},{0,2},{1,3},{6,4},{7,5},{4,6},{5,7},{10,8},{11,9},{8,1... | collective-permute-start | bytes 442376 | tf_op jit(solution)/shard_map/ppermute | solution.py:34
  345.3 8.7 %collective-permute-start.72 = (bf16[96,768]{1,0:T(8,128)(2,1)S(1)}, bf16[96,768]{1,0:T(8,128)(2,1)S(1)}, u32[]{:S(2)}, u32[]{:S(2)}) collective-permute-start(bf16[96,768]{1,0:T(8,128)(2,1)S(1)} %get-tuple-element.92), channel_id=1, source_target_pairs={{3,0},{0,1},{1,2},{2,3},{7,4},{4,5},{5,6},{6,7},{11,8},{8,9},{9,10... | collective-permute-start | bytes 442376 | tf_op jit(solution)/shard_map/ppermute | solution.py:34
  370.7 107.1 %collective-permute-start.44 = (bf16[576,768]{1,0:T(8,128)(2,1)S(1)}, bf16[576,768]{1,0:T(8,128)(2,1)}, u32[]{:S(2)}, u32[]{:S(2)}) collective-permute-start(bf16[576,768]{1,0:T(8,128)(2,1)S(1)} %bitcast.504), channel_id=1, source_target_pairs={{64,0},{65,1},{66,2},{67,3},{68,4},{69,5},{70,6},{71,7},{72,8},{73... | collective-permute-start | bytes 2654216 | tf_op jit(solution)/shard_map/ppermute | solution.py:34
  373.6 105.6 %collective-permute-start.45 = (bf16[576,768]{1,0:T(8,128)(2,1)S(1)}, bf16[576,768]{1,0:T(8,128)(2,1)}, u32[]{:S(2)}, u32[]{:S(2)}) collective-permute-start(bf16[576,768]{1,0:T(8,128)(2,1)S(1)} %bitcast.505), channel_id=1, source_target_pairs={{96,0},{97,1},{98,2},{99,3},{100,4},{101,5},{102,6},{103,7},{104,8... | collective-permute-start | bytes 2654216 | tf_op jit(solution)/shard_map/ppermute | solution.py:34
  397.4 13.0 %collective-permute-start.80 = (bf16[24,768]{1,0:T(8,128)(2,1)S(1)}, bf16[24,768]{1,0:T(8,128)(2,1)S(1)}, u32[]{:S(2)}, u32[]{:S(2)}) collective-permute-start(bf16[24,768]{1,0:T(8,128)(2,1)S(1)} %get-tuple-element.58), channel_id=1, source_target_pairs={{96,0},{97,1},{98,2},{99,3},{100,4},{101,5},{102,6},{103,7},{104,8... | collective-permute-start | bytes 110600 | tf_op jit(solution)/shard_map/ppermute | solution.py:34
  441.1 6.9 %collective-permute-start.81 = (bf16[96,768]{1,0:T(8,128)(2,1)S(1)}, bf16[96,768]{1,0:T(8,128)(2,1)S(1)}, u32[]{:S(2)}, u32[]{:S(2)}) collective-permute-start(bf16[96,768]{1,0:T(8,128)(2,1)S(1)} %bitcast.557), channel_id=1, source_target_pairs={{1,0},{2,1},{3,2},{0,3},{5,4},{6,5},{7,6},{4,7},{9,8},{10,9},{11,1... | collective-permute-start | bytes 442376 | tf_op jit(solution)/shard_map/ppermute | solution.py:34
  444.4 6.7 %collective-permute-start.82 = (bf16[96,768]{1,0:T(8,128)(2,1)S(1)}, bf16[96,768]{1,0:T(8,128)(2,1)S(1)}, u32[]{:S(2)}, u32[]{:S(2)}) collective-permute-start(bf16[96,768]{1,0:T(8,128)(2,1)S(1)} %bitcast.558), channel_id=1, source_target_pairs={{2,0},{3,1},{0,2},{1,3},{6,4},{7,5},{4,6},{5,7},{10,8},{11,9},{8,1... | collective-permute-start | bytes 442376 | tf_op jit(solution)/shard_map/ppermute | solution.py:34
  456.7 7.1 %collective-permute-start.104 = (bf16[96,768]{1,0:T(8,128)(2,1)S(1)}, bf16[96,768]{1,0:T(8,128)(2,1)S(1)}, u32[]{:S(2)}, u32[]{:S(2)}) collective-permute-start(bf16[96,768]{1,0:T(8,128)(2,1)S(1)} %bitcast.549), channel_id=1, source_target_pairs={{96,0},{97,1},{98,2},{99,3},{100,4},{101,5},{102,6},{103,7},{104,8... | collective-permute-start | bytes 442376 | tf_op jit(solution)/shard_map/ppermute | solution.py:34
  470.4 47.8 %collective-permute-start.15 = (bf16[4,256,384]{1,2,0:T(8,128)(2,1)}, bf16[4,256,384]{1,2,0:T(8,128)(2,1)}, u32[]{:S(2)}, u32[]{:S(2)}) collective-permute-start(bf16[4,256,384]{1,2,0:T(8,128)(2,1)} %slice_bitcast_fusion), channel_id=1, source_target_pairs={{16,0},{17,1},{18,2},{19,3},{20,4},{21,5},{22,6},{23,7},{24,8},{25... | collective-permute-start | bytes 2359304 | tf_op jit(solution)/shard_map/ppermute | solution.py:34
  471.9 26.1 %collective-permute-start.84 = (bf16[384,768]{1,0:T(8,128)(2,1)S(1)}, bf16[384,768]{1,0:T(8,128)(2,1)}, u32[]{:S(2)}, u32[]{:S(2)}) collective-permute-start(bf16[384,768]{1,0:T(8,128)(2,1)S(1)} %bitcast.517), channel_id=1, source_target_pairs={{4,0},{5,1},{6,2},{7,3},{16,4},{17,5},{18,6},{19,7},{12,8},{13,9},... | collective-permute-start | bytes 1769480 | tf_op jit(solution)/shard_map/ppermute | solution.py:34
  474.0 27.2 %collective-permute-start.85 = (bf16[384,768]{1,0:T(8,128)(2,1)S(1)}, bf16[384,768]{1,0:T(8,128)(2,1)}, u32[]{:S(2)}, u32[]{:S(2)}) collective-permute-start(bf16[384,768]{1,0:T(8,128)(2,1)S(1)} %bitcast.518), channel_id=1, source_target_pairs={{16,0},{17,1},{18,2},{19,3},{20,4},{21,5},{22,6},{23,7},{24,8},{25... | collective-permute-start | bytes 1769480 | tf_op jit(solution)/shard_map/ppermute | solution.py:34
  477.8 27.6 %collective-permute-start.86 = (bf16[384,768]{1,0:T(8,128)(2,1)S(1)}, bf16[384,768]{1,0:T(8,128)(2,1)}, u32[]{:S(2)}, u32[]{:S(2)}) collective-permute-start(bf16[384,768]{1,0:T(8,128)(2,1)S(1)} %bitcast.519), channel_id=1, source_target_pairs={{20,0},{21,1},{22,2},{23,3},{0,4},{1,5},{2,6},{3,7},{28,8},{29,9},... | collective-permute-start | bytes 1769480 | tf_op jit(solution)/shard_map/ppermute | solution.py:34
  479.1 36.2 %collective-permute-start.105 = (bf16[384,768]{1,0:T(8,128)(2,1)S(1)}, bf16[384,768]{1,0:T(8,128)(2,1)}, u32[]{:S(2)}, u32[]{:S(2)}) collective-permute-start(bf16[384,768]{1,0:T(8,128)(2,1)S(1)} %bitcast.512), channel_id=1, source_target_pairs={{1,0},{2,1},{3,2},{0,3},{5,4},{6,5},{7,6},{4,7},{9,8},{10,9},{11,1... | collective-permute-start | bytes 1769480 | tf_op jit(solution)/shard_map/ppermute | solution.py:34
  498.0 19.0 %collective-permute-start.106 = (bf16[384,768]{1,0:T(8,128)(2,1)S(1)}, bf16[384,768]{1,0:T(8,128)(2,1)S(1)}, u32[]{:S(2)}, u32[]{:S(2)}) collective-permute-start(bf16[384,768]{1,0:T(8,128)(2,1)S(1)} %bitcast.513), channel_id=1, source_target_pairs={{2,0},{3,1},{0,2},{1,3},{6,4},{7,5},{4,6},{5,7},{10,8},{11,9},{8,1... | collective-permute-start | bytes 1769480 | tf_op jit(solution)/shard_map/ppermute | solution.py:34
  501.2 15.8 %collective-permute-start.107 = (bf16[384,768]{1,0:T(8,128)(2,1)S(1)}, bf16[384,768]{1,0:T(8,128)(2,1)S(1)}, u32[]{:S(2)}, u32[]{:S(2)}) collective-permute-start(bf16[384,768]{1,0:T(8,128)(2,1)S(1)} %bitcast.514), channel_id=1, source_target_pairs={{3,0},{0,1},{1,2},{2,3},{7,4},{4,5},{5,6},{6,7},{11,8},{8,9},{9,10... | collective-permute-start | bytes 1769480 | tf_op jit(solution)/shard_map/ppermute | solution.py:34
  505.3 42.2 %collective-permute-start.66 = (bf16[384,768]{1,0:T(8,128)(2,1)}, bf16[384,768]{1,0:T(8,128)(2,1)}, u32[]{:S(2)}, u32[]{:S(2)}) collective-permute-start(bf16[384,768]{1,0:T(8,128)(2,1)} %bitcast.132), channel_id=1, source_target_pairs={{8,0},{9,1},{10,2},{11,3},{12,4},{13,5},{14,6},{15,7},{0,8},{1,9},... | collective-permute-start | bytes 1769480 | tf_op jit(solution)/shard_map/ppermute | solution.py:34
  515.3 59.0 %collective-permute-start.87 = (bf16[1536,768]{1,0:T(8,128)(2,1)}, bf16[1536,768]{1,0:T(8,128)(2,1)}, u32[]{:S(2)}, u32[]{:S(2)}) collective-permute-start(bf16[1536,768]{1,0:T(8,128)(2,1)} %bitcast.167), channel_id=1, source_target_pairs={{8,0},{9,1},{10,2},{11,3},{12,4},{13,5},{14,6},{15,7},{0,8},{1,9},... | collective-permute-start | bytes 7077896 | tf_op jit(solution)/shard_map/ppermute | solution.py:34
  519.6 15.4 %collective-permute-start.16 = (bf16[256,576]{0,1:T(8,128)(2,1)S(1)}, bf16[256,576]{0,1:T(8,128)(2,1)S(1)}, u32[]{:S(2)}, u32[]{:S(2)}) collective-permute-start(bf16[256,576]{0,1:T(8,128)(2,1)S(1)} %get-tuple-element.85), channel_id=1, source_target_pairs={{32,0},{33,1},{34,2},{35,3},{36,4},{37,5},{38,6},{39,7},{40,8},{41... | collective-permute-start | bytes 884744 | tf_op jit(solution)/shard_map/ppermute | solution.py:34
  521.2 13.9 %collective-permute-start.17 = (bf16[256,576]{0,1:T(8,128)(2,1)S(1)}, bf16[256,576]{0,1:T(8,128)(2,1)S(1)}, u32[]{:S(2)}, u32[]{:S(2)}) collective-permute-start(bf16[256,576]{0,1:T(8,128)(2,1)S(1)} %get-tuple-element.86), channel_id=1, source_target_pairs={{64,0},{65,1},{66,2},{67,3},{68,4},{69,5},{70,6},{71,7},{72,8},{73... | collective-permute-start | bytes 884744 | tf_op jit(solution)/shard_map/ppermute | solution.py:34
  522.9 71.0 %collective-permute-start.108 = (bf16[1536,768]{1,0:T(8,128)(2,1)}, bf16[1536,768]{1,0:T(8,128)(2,1)}, u32[]{:S(2)}, u32[]{:S(2)}) collective-permute-start(bf16[1536,768]{1,0:T(8,128)(2,1)} %bitcast.203), channel_id=1, source_target_pairs={{8,0},{9,1},{10,2},{11,3},{12,4},{13,5},{14,6},{15,7},{0,8},{1,9},... | collective-permute-start | bytes 7077896 | tf_op jit(solution)/shard_map/ppermute | solution.py:34
  535.1 8.2 %collective-permute-start.18 = (bf16[256,576]{0,1:T(8,128)(2,1)S(1)}, bf16[256,576]{0,1:T(8,128)(2,1)S(1)}, u32[]{:S(2)}, u32[]{:S(2)}) collective-permute-start(bf16[256,576]{0,1:T(8,128)(2,1)S(1)} %get-tuple-element.83), channel_id=1, source_target_pairs={{96,0},{97,1},{98,2},{99,3},{100,4},{101,5},{102,6},{103,7},{104,8... | collective-permute-start | bytes 884744 | tf_op jit(solution)/shard_map/ppermute | solution.py:34
  (84 other events, 653.9 us)
